TPU v7x, 32 devices: a whole 2x2x4 slice. The times are simulated.
32 devices in a mesh: wide: 8 (over z, x), narrow: 4 (over y, core).
Axes of the slice: x: 2, y: 2, z: 4, core: 2. Of those that a mesh axis runs over, the one named last changes fastest.
Arguments:
- frames: bfloat16 [8, 512, 1024], P('wide', 'narrow'), may hold values from -6 to 6
- out_grad: bfloat16 [8, 512, 1024], P('wide', 'narrow'), may hold values from -6 to 6
- qkv_weight: bfloat16 [1024, 3072], P(('wide', 'narrow')), may hold values from -0.1875 to 0.1875
- out_weight: bfloat16 [1024, 1024], P(('wide', 'narrow')), may hold values from -0.75 to 0.75
- gate_up_weight: bfloat16 [1024, 8192], P(('wide', 'narrow')), may hold values from -0.1875 to 0.1875
- down_weight_t: bfloat16 [1024, 4096], P(('wide', 'narrow')), may hold values from -0.09375 to 0.09375
- norm_gain_one: float32 [1024], replicated, may hold values from 0.5 to 1.5
- norm_gain_two: float32 [1024], replicated, may hold values from 0.5 to 1.5
- layer_scale_one: float32 [1024], replicated, may hold values from 0.5 to 1.5
- layer_scale_two: float32 [1024], replicated, may hold values from 0.5 to 1.5
- speaker: int32 [8], P('wide'), may hold values from 0 to 127
- clip_bounds: int32 [8, 2], P('wide'), may hold values from 1 to 512, as said below
Outputs:
- output: bfloat16 [8, 512, 1024], P('wide', 'narrow')
- speaker_power: float32 [128, 1024], replicated
- frames_grad: bfloat16 [8, 512, 1024], P('wide', 'narrow')
- qkv_weight_grad: float32 [1024, 3072], P('wide', 'narrow')
- out_weight_grad: float32 [1024, 1024], P('wide', 'narrow')
- gate_up_weight_grad: float32 [1024, 8192], P('wide', 'narrow')
- down_weight_grad: float32 [1024, 4096], P('wide', 'narrow')
- norm_gain_one_grad: float32 [1024], replicated
- norm_gain_two_grad: float32 [1024], replicated
- layer_scale_one_grad: float32 [1024], replicated
- layer_scale_two_grad: float32 [1024], replicated
Inputs may be any that keep to these rules, and one draw needn't show every extreme that they name: Each stream holds at most three clips; clip_bounds[s, 0] < clip_bounds[s, 1] (a third clip is empty when its start is 512). In each block of 1 streams, one stream drawn from the seed has its second clip start before frame 128 and its third after frame 512 - 128; in the first block that stream's bounds are 1 and 512.
All inputs are finite; a program needn't handle non-finite values.
Results may differ from a plain program's by a relative error of at most 0.015.
Values may be sent and summed in bfloat16 or wider, within the bound.
No kernel may reach another device: no remote copies, remote signals or barrier semaphores. Data moves between devices by JAX's collectives and lax.ppermute only.
A program may use at most 192 MiB of HBM per device.

v0:
```python
import functools
import math

import jax
import jax.numpy as jnp
from jax import lax
from jax.experimental import pallas as pl
from jax.experimental.pallas import tpu as pltpu
from jax.sharding import Mesh, PartitionSpec as P

HEADS = 16
WINDOW = 128
CLIP_LEN = 512
SPEAKERS = 128

bf16 = jnp.bfloat16
f32 = jnp.float32
highest = lax.Precision.HIGHEST

FAR, NEAR, PAIR, CORE = "far", "near", "pair", "core"
ALL = (FAR, NEAR, PAIR, CORE)
SWAP = [(0, 1), (1, 0)]


def swap(x, axis):
    return lax.ppermute(x, axis, SWAP)


def dot(a, b):
    return jnp.dot(a, b, preferred_element_type=f32)


def dot_t(a, b):
    return lax.dot_general(a, b, (((1,), (1,)), ((), ())), preferred_element_type=f32)


def tdot(a, b):
    return lax.dot_general(a, b, (((0,), (0,)), ((), ())), preferred_element_type=f32)


def far_count():
    return lax.axis_size(FAR)


def piece_index():
    far, near = lax.axis_index(FAR), lax.axis_index(NEAR)
    return [(far ^ k) * 2 + (near ^ i) for i in range(2) for k in range(far_count())]


def to_pieces(x, axis):
    size = x.shape[axis] // (2 * far_count())
    return jnp.concatenate(
        [lax.dynamic_slice_in_dim(x, i * size, size, axis) for i in piece_index()], axis=axis
    )


def from_pieces(x, axis):
    count = far_count()
    far, near = lax.axis_index(FAR), lax.axis_index(NEAR)
    size = x.shape[axis] // (2 * count)
    return jnp.concatenate(
        [
            lax.dynamic_slice_in_dim(x, ((near ^ i) * count + (far ^ k)) * size, size, axis)
            for k in range(count)
            for i in range(2)
        ],
        axis=axis,
    )


def swap_far(x, bit):
    return lax.ppermute(x, FAR, [(i, i ^ bit) for i in range(far_count())])


def gather_line(block):
    own = [block]
    for j in range(1, far_count()):
        low = j & -j
        own.append(swap_far(own[j ^ low], low))
    return own


def gather_rows(block):
    own = gather_line(block)
    return own + [swap(x, NEAR) for x in own]


def scatter_parts(parts):
    count = far_count()
    total = [
        parts[0, k] + swap(parts[1, k].astype(bf16), NEAR).astype(f32) for k in range(count)
    ]
    for j in range(count - 1, 0, -1):
        low = j & -j
        total[j ^ low] = total[j ^ low] + swap_far(total[j].astype(bf16), low).astype(f32)
    return total[0]


def core_columns(x):
    core = lax.axis_index(CORE)
    slices = [[x[0], x[1]], [x[2], x[3]]]
    stay = jnp.stack([jnp.where(core == 0, s[0], s[1]) for s in slices])
    send = jnp.stack([jnp.where(core == 0, s[1], s[0]) for s in slices])
    got = swap(send, CORE)
    return jnp.concatenate([jnp.where(core == 0, stay, got), jnp.where(core == 0, got, stay)], axis=1)


def pair_columns(x):
    pair = lax.axis_index(PAIR)
    stay = jnp.where(pair == 0, x[0], x[1])
    got = swap(jnp.where(pair == 0, x[1], x[0]), PAIR)
    return jnp.concatenate([jnp.where(pair == 0, stay, got), jnp.where(pair == 0, got, stay)], axis=0)


BLOCK = 128
PIECES = 8
LINE = 4
MICROSECONDS = dict(
    attend=9, residual=3, mlp=11, middle=2, finish=2, attend_back=11, last=2, rows=1, onward=1, merge=1, weight_grad=2,
    fence=1, tick=0, totals=1, out=0,
)
RATE = 10**8


def call(kernel, name, outs, ins, scratch=(), smem=0, anywhere=(), far_outs=(), megabytes=24, after=()):
    specs = []
    given = len(ins)
    if len(after) > 0:
        inner = kernel

        def kernel(*refs):
            inner(*refs[:given], *refs[given + len(after) :])

    for i in range(len(ins)):
        if i < smem:
            specs.append(pl.BlockSpec(memory_space=pltpu.SMEM))
        elif i in anywhere:
            specs.append(pl.BlockSpec(memory_space=pltpu.HBM))
        else:
            specs.append(pl.BlockSpec(memory_space=pltpu.VMEM))
    specs += [pl.BlockSpec(memory_space=pl.ANY)] * len(after)
    return pl.pallas_call(
        kernel,
        out_shape=[jax.ShapeDtypeStruct(shape, dtype) for shape, dtype in outs],
        in_specs=specs,
        out_specs=[
            pl.BlockSpec(memory_space=pltpu.HBM if i in far_outs else pltpu.VMEM) for i in range(len(outs))
        ],
        scratch_shapes=list(scratch),
        compiler_params=pltpu.CompilerParams(vmem_limit_bytes=megabytes * 2**20),
        cost_estimate=pl.CostEstimate(
            flops=int(MICROSECONDS[name] * RATE), bytes_accessed=0, transcendentals=0
        ),
        name=name,
    )(*ins, *after)


def wide_here():
    if lax.axis_size(FAR) != LINE:
        return 0
    return lax.axis_index(FAR) * 2 + lax.axis_index(NEAR)


def far_here():
    return lax.axis_index(FAR) if lax.axis_size(FAR) == LINE else 0


def shard_here():
    return lax.axis_index(PAIR) * 2 + lax.axis_index(CORE)


def feature_block(wide, piece):
    return wide ^ ((piece % 4) * 2 + piece // 4)


def lanes(block, size=BLOCK):
    return pl.ds(pl.multiple_of(block * size, size), size)


def normalise(x):
    centred = x - jnp.mean(x, axis=1, keepdims=True)
    inverse = lax.rsqrt(jnp.mean(centred * centred, axis=1, keepdims=True) + 1e-05)
    return centred * inverse, inverse


def turn(x, cos, sin, sign):
    lane = lax.broadcasted_iota(jnp.int32, x.shape, 1)
    lower = (lane & 63) < 32
    partner = jnp.where(lower, pltpu.roll(x, BLOCK - 32, 1), pltpu.roll(x, 32, 1))
    return x * cos + (sign * partner) * sin


def allowed_pairs(shard, block, first, second, keys):
    row = lax.broadcasted_iota(jnp.int32, (BLOCK, keys), 0)
    lane = lax.broadcasted_iota(jnp.int32, (BLOCK, keys), 1)
    query = (shard ^ block) * BLOCK + row
    key = (shard ^ (lane // BLOCK)) * BLOCK + lane % BLOCK

    def segment(position):
        return (position >= first).astype(jnp.int32) + (position >= second).astype(jnp.int32)

    return (jnp.abs(query - key) <= WINDOW) & (segment(query) == segment(key))


def half_mask(head, shape):
    lane = lax.broadcasted_iota(jnp.int32, shape, 1)
    return (lane // 64) == head


def out_kernel(*refs):
    pieces, (out, sems) = refs[:PIECES], refs[PIECES:]
    group = out.shape[1]
    copies = [
        pltpu.make_async_copy(
            pieces[j].at[:, pl.ds(3 * group, group)],
            out.at[lanes(feature_block(wide_here(), j)), :],
            sems.at[j],
        )
        for j in range(PIECES)
    ]
    for copy in copies:
        copy.start()
    for copy in copies:
        copy.wait()


def attend_kernel(bounds, own, core, across, both, *refs):
    pieces = refs[:PIECES]
    gain, cos, sin, normed, qkv, stat, att, att_core, att_pair, weight, sems = refs[PIECES:]
    wide, shard, first, second = wide_here(), shard_here(), bounds[0, 0], bounds[0, 1]
    group = att.shape[1]
    copies = [
        pltpu.make_async_copy(
            pieces[j].at[:, pl.ds(0, 3 * group)], weight.at[lanes(feature_block(wide, j)), :], sems.at[j]
        )
        for j in range(PIECES)
    ]
    for copy in copies:
        copy.start()
    for b, x in enumerate((own, core, across, both)):
        unit, _ = normalise(x[...].astype(f32))
        normed[b * BLOCK : (b + 1) * BLOCK, :] = (unit * gain[...]).astype(bf16)
    for copy in copies:
        copy.wait()
    tiles = group // BLOCK
    for part in range(3):
        x = dot(normed[...], weight[:, part * group : (part + 1) * group])
        for t in range(tiles):
            y = x[:, t * BLOCK : (t + 1) * BLOCK]
            if part < 2:
                y = turn(y, cos[...], sin[...], 1.0)
            at = part * group + t * BLOCK
            qkv[:, at : at + BLOCK] = y.astype(bf16)
    keys = normed.shape[0]
    scale = 64**-0.5
    for b in range(4):
        here = slice(b * BLOCK, (b + 1) * BLOCK)
        mask = allowed_pairs(shard, b, first, second, keys)
        stats = jnp.zeros((BLOCK, BLOCK), f32)
        for t in range(tiles):
            query = qkv[here, t * BLOCK : (t + 1) * BLOCK]
            key = qkv[:, group + t * BLOCK : group + (t + 1) * BLOCK]
            value = qkv[:, 2 * group + t * BLOCK : 2 * group + (t + 1) * BLOCK]
            merged = None
            for h in range(2):
                keep = half_mask(h, query.shape)
                scores = dot_t(jnp.where(keep, query, jnp.zeros_like(query)), key) * scale
                scores = jnp.where(mask, scores, -1e30)
                peak = jnp.max(scores, axis=1, keepdims=True)
                exponent = jnp.exp(scores - peak)
                total = jnp.sum(exponent, axis=1, keepdims=True)
                probs = (exponent * (1.0 / total)).astype(bf16)
                lane = lax.broadcasted_iota(jnp.int32, stats.shape, 1)
                stats = jnp.where(lane == 2 * t + h, peak + jnp.log(total), stats)
                part = dot(probs, value)
                merged = part if merged is None else jnp.where(keep, part, merged)
            merged = merged.astype(bf16)
            cols = slice(t * BLOCK, (t + 1) * BLOCK)
            att[here, cols] = merged
            to_core, to_pair = b ^ 1, b ^ 2
            att_core[to_core * BLOCK : (to_core + 1) * BLOCK, cols] = merged
            att_pair[to_pair * BLOCK : (to_pair + 1) * BLOCK, cols] = merged
        stat[here, :] = stats


def residual_kernel(
    own, core, across, both, att0, att1, att2, att3, out0, out1, out2, out3, scale_one, gain_two,
    normed, normed_even, attended, residual_own, branch_own, branch,
):
    shard = shard_here()
    group = out0.shape[1]
    for m, part in enumerate((att0, att1)):
        attended[:, lanes(shard ^ m, group)] = part[...]
    attended[:, lanes(shard ^ 2, group)] = att2[...]
    for b in range(4):
        attended[b * BLOCK : (b + 1) * BLOCK, lanes(shard ^ 3, group)] = att3[
            (b ^ 1) * BLOCK : ((b ^ 1) + 1) * BLOCK, :
        ]
    for m, part in enumerate((out0, out1, out2, out3)):
        branch[:, lanes(shard ^ m, group)] = dot(attended[...], part[...])
    for b, x in enumerate((own, core, across, both)):
        here = slice(b * BLOCK, (b + 1) * BLOCK)
        total = x[...].astype(f32) + scale_one[...] * branch[here, :]
        unit, _ = normalise(total)
        low = (unit * gain_two[...]).astype(bf16)
        normed[here, :] = low
        if b % 2 == 0:
            normed_even[b // 2 * BLOCK : (b // 2 + 1) * BLOCK, :] = low
        if b == 0:
            residual_own[...] = total
            branch_own[...] = branch[here, :]


def mlp_kernel(normed_here, near_even, near_odd, *refs):
    grads, refs = refs[:8], refs[8:]
    pieces, scale_two, refs = refs[:LINE], refs[LINE], refs[LINE + 1 :]
    (keep, send, keep_late, send_late), outs, refs = refs[:4], refs[4 : 4 + LINE], refs[4 + LINE :]
    normed, mlp_grad, activated, gate_up_grad, weight, sems = refs
    far = far_here()
    rows = pieces[0].shape[0]
    copies = [
        pltpu.make_async_copy(pieces[k], weight.at[lanes(far ^ k, rows), :], sems.at[k]) for k in range(LINE)
    ]
    for copy in copies:
        copy.start()
    tokens = 4 * BLOCK
    normed[:tokens, :] = normed_here[...]
    for b in range(4):
        source = near_odd if b % 2 else near_even
        normed[tokens + b * BLOCK : tokens + (b + 1) * BLOCK, :] = source[b // 2 * BLOCK : (b // 2 + 1) * BLOCK, :]
    for b, x in enumerate(grads):
        mlp_grad[b * BLOCK : (b + 1) * BLOCK, :] = (scale_two[...] * x[...].astype(f32)).astype(bf16)
    for copy in copies:
        copy.wait()
    hidden = activated.shape[1]
    gate_at, up_at, down_at = [slice(i * hidden, (i + 1) * hidden) for i in range(3)]
    for stream in range(2):
        here = slice(stream * tokens, (stream + 1) * tokens)
        gate = dot(normed[here, :], weight[:, gate_at])
        up = dot(normed[here, :], weight[:, up_at])
        act_grad = dot(mlp_grad[here, :], weight[:, down_at])
        sigmoid = 1.0 / (1.0 + jnp.exp(-gate))
        silu = gate * sigmoid
        activated[here, :] = (silu * up).astype(bf16)
        gate_up_grad[here, gate_at] = (act_grad * up * sigmoid * (1.0 + gate * (1.0 - sigmoid))).astype(bf16)
        gate_up_grad[here, up_at] = (act_grad * silu).astype(bf16)
        back = dot_t(gate_up_grad[here, gate_at], weight[:, gate_at])
        back = (back + dot_t(gate_up_grad[here, up_at], weight[:, up_at])).astype(bf16)
        branch = dot_t(activated[here, :], weight[:, down_at]).astype(bf16)
        for b in range(4):
            here = slice(b * BLOCK, (b + 1) * BLOCK)
            at = stream * 2 * BLOCK + b // 2 * BLOCK
            early, late = (send, send_late) if b % 2 else (keep, keep_late)
            early[at : at + BLOCK, :] = back[here, :]
            late[at : at + BLOCK, :] = branch[here, :]
    for k, out in enumerate(outs):
        cols = lanes(far ^ k, rows)
        out[:, : 2 * hidden] = tdot(normed[:, cols], gate_up_grad[...]).astype(bf16)
        out[:, 2 * hidden :] = tdot(mlp_grad[:, cols], activated[...]).astype(bf16)


def near_kernel(keep, got, out):
    half = 2 * BLOCK
    out[...] = (keep[half:, :].astype(f32) + got[half:, :].astype(f32)).astype(bf16)


def pair_kernel(keep, got, got_near, out):
    at = slice(BLOCK, 2 * BLOCK)
    out[...] = (keep[at, :].astype(f32) + got[at, :].astype(f32) + got_near[at, :].astype(f32)).astype(bf16)


def own_sum(keep, got, got_near, got_pair):
    terms = (got, got_near, got_pair)
    total = keep[:BLOCK, :].astype(f32)
    for term in terms:
        total = total + term[:BLOCK, :].astype(f32)
    return total


def onward_kernel(keep, got, out):
    out[...] = (keep[BLOCK:, :] + got[BLOCK:, :].astype(f32)).astype(bf16)


def middle_kernel(
    keep, got, got_near, got_pair, own_grad, residual, branch_one, scale_one, gain_two,
    residual_grad, attn_grad, rows,
):
    incoming = own_sum(keep, got, got_near, got_pair)
    grad = own_grad[...].astype(f32)
    unit, inverse = normalise(residual[...])
    scaled = incoming * gain_two[...]
    back = inverse * (
        scaled
        - jnp.mean(scaled, axis=1, keepdims=True)
        - unit * jnp.mean(scaled * unit, axis=1, keepdims=True)
    )
    total = grad + back
    residual_grad[...] = total
    attn_grad[...] = (scale_one[...] * total).astype(bf16)
    rows[...] = jnp.zeros(rows.shape, f32)
    rows[2:3, :] = jnp.sum(incoming * unit, axis=0, keepdims=True)
    rows[3:4, :] = jnp.sum(total * branch_one[...], axis=0, keepdims=True)


def finish_kernel(
    speaker, keep, got, got_near, got_pair, own_grad, residual, rows_in, scale_two, output, spread
):
    branch_two = own_sum(keep, got, got_near, got_pair)
    result = residual[...] + scale_two[...] * branch_two
    output[...] = result.astype(bf16)
    width = residual.shape[1]
    power = jnp.sum(result * result, axis=0, keepdims=True)
    scale_grad = jnp.sum(own_grad[...].astype(f32) * branch_two, axis=0, keepdims=True)
    for i in range(spread.shape[0]):
        spread[i, 0:1, :] = power
        spread[i, 1:2, :] = scale_grad
        spread[i, 2:4, :] = rows_in[2:4, :]
        spread[i, 4:5, :] = jnp.full((1, width), speaker[0], jnp.int32).astype(f32)


def attend_back_kernel(bounds, own, core, across, both, qkv, stat, cos, sin, *refs):
    outs, pieces, lefts, refs = refs[:4], refs[4 : 4 + PIECES], refs[4 + PIECES : 6 + PIECES], refs[6 + PIECES :]
    (keep, send), products, refs = refs[:2], refs[2 : 2 + PIECES], refs[2 + PIECES :]
    projected, weight, grads, att_grad, probs_all, score_all, parts, normed, attended, sems = refs
    wide, shard, first, second = wide_here(), shard_here(), bounds[0, 0], bounds[0, 1]
    group = parts.shape[2]
    out_copies = [
        pltpu.make_async_copy(outs[m].at[lanes(shard, group), :], parts.at[m], sems.at[m]) for m in range(4)
    ]
    copies = [
        pltpu.make_async_copy(
            pieces[j].at[:, pl.ds(0, 3 * group)], weight.at[lanes(feature_block(wide, j)), :], sems.at[4 + j]
        )
        for j in range(PIECES)
    ]
    copies += [
        pltpu.make_async_copy(left, here, sems.at[4 + PIECES + i])
        for i, (left, here) in enumerate(zip(lefts, (normed, attended)))
    ]
    for copy in out_copies + copies:
        copy.start()
    for b, x in enumerate((own, core, across, both)):
        grads[b * BLOCK : (b + 1) * BLOCK, :] = x[...]
    for copy in out_copies:
        copy.wait()
    tiles = group // BLOCK
    total = None
    for m in range(4):
        product = dot_t(grads[:, lanes(shard ^ m, group)], parts[m])
        total = product if total is None else total + product
    att_grad[...] = total.astype(bf16)
    keys = qkv.shape[0]
    scale = 64**-0.5
    for t in range(tiles):
        cols = slice(t * BLOCK, (t + 1) * BLOCK)
        key = qkv[:, group + t * BLOCK : group + (t + 1) * BLOCK]
        value = qkv[:, 2 * group + t * BLOCK : 2 * group + (t + 1) * BLOCK]
        query_grad = [None] * 4
        key_grad = None
        value_grad = None
        for h in range(2):
            for b in range(4):
                here = slice(b * BLOCK, (b + 1) * BLOCK)
                mask = allowed_pairs(shard, b, first, second, keys)
                query = qkv[here, cols]
                grad = att_grad[here, cols]
                keep_lanes = half_mask(h, query.shape)
                none = jnp.zeros_like(query)
                scores = dot_t(jnp.where(keep_lanes, query, none), key) * scale
                probs = jnp.where(mask, jnp.exp(scores - stat[here, 2 * t + h : 2 * t + h + 1]), 0.0)
                grad_here = jnp.where(keep_lanes, grad, none)
                prob_grad = dot_t(grad_here, value)
                delta = jnp.sum(probs * prob_grad, axis=1, keepdims=True)
                score_grad = (probs * (prob_grad - delta)).astype(bf16)
                probs_all[here, :] = probs.astype(bf16)
                score_all[here, :] = score_grad
                part = dot(score_grad, key)
                query_grad[b] = part if h == 0 else jnp.where(keep_lanes, part, query_grad[b])
            k_part = tdot(score_all[...], qkv[:, cols])
            v_part = tdot(probs_all[...], att_grad[:, cols])
            keep_all = half_mask(h, k_part.shape)
            key_grad = k_part if h == 0 else jnp.where(keep_all, k_part, key_grad)
            value_grad = v_part if h == 0 else jnp.where(keep_all, v_part, value_grad)
        for b in range(4):
            here = slice(b * BLOCK, (b + 1) * BLOCK)
            projected[here, cols] = turn(
                query_grad[b] * scale, cos[here, :], sin[here, :], -1.0
            ).astype(bf16)
        projected[:, group + t * BLOCK : group + (t + 1) * BLOCK] = turn(
            key_grad * scale, cos[...], sin[...], -1.0
        ).astype(bf16)
        projected[:, 2 * group + t * BLOCK : 2 * group + (t + 1) * BLOCK] = value_grad.astype(bf16)
    for copy in copies:
        copy.wait()
    for b, target in enumerate((keep, send, keep, send)):
        at = (b // 2) * BLOCK
        target[at : at + BLOCK, :] = dot_t(
            projected[b * BLOCK : (b + 1) * BLOCK, :], weight[...]
        ).astype(target.dtype)
    for j, out in enumerate(products):
        cols = lanes(feature_block(wide, j))
        out[:, : 3 * group] = tdot(normed[:, cols], projected[...]).astype(bf16)
        out[:, 3 * group :] = tdot(attended[:, cols], grads[:, lanes(shard, group)]).astype(bf16)


def last_kernel(keep, got_core, got_pair, frames, residual_grad, gain_one, frames_grad, spread):
    incoming = keep[:BLOCK, :] + got_core[:BLOCK, :].astype(f32) + got_pair[...].astype(f32)
    unit, inverse = normalise(frames[...].astype(f32))
    scaled = incoming * gain_one[...]
    back = inverse * (
        scaled
        - jnp.mean(scaled, axis=1, keepdims=True)
        - unit * jnp.mean(scaled * unit, axis=1, keepdims=True)
    )
    frames_grad[...] = (residual_grad[...] + back).astype(bf16)
    row = jnp.sum(incoming * unit, axis=0, keepdims=True)
    for i in range(spread.shape[0]):
        spread[i] = row


def copy_kernel(*refs):
    count = len(refs) // 2
    for source, target in zip(refs[:count], refs[count:]):
        target[...] = source[...]


def tick_kernel(out):
    out[...] = jnp.zeros(out.shape, f32)


def hops(x, count):
    def tick(after):
        return call(tick_kernel, "tick", [((8, BLOCK), f32)], [], after=[after])[0]

    small = tick(x)
    for _ in range(count):
        small = tick(swap(small, CORE))
    return small


def merge_kernel(terms, outs):
    total = terms[0][...].astype(f32)
    for term in terms[1:]:
        total = total + term[...].astype(f32)
    at = 0
    for out in outs:
        out[...] = total[:, at : at + out.shape[1]].astype(out.dtype)
        at += out.shape[1]


def merge(terms, outs, after=()):
    count = len(terms)
    return call(
        lambda *refs: merge_kernel(refs[:count], refs[count:]),
        "merge",
        [((terms[0].shape[0], width), dtype) for width, dtype in outs],
        terms,
        after=after,
    )


def split_rows_kernel(terms, outs):
    near = lax.axis_index(NEAR)
    rows = outs[0].shape[0]
    for out, whose in zip(outs, (near, 1 - near)):
        here = pl.ds(pl.multiple_of(whose * rows, rows), rows)
        total = terms[0][here, :].astype(f32)
        for term in terms[1:]:
            total = total + term[here, :].astype(f32)
        out[...] = total.astype(out.dtype)


def totals_kernel(rows, power, gain, one, two):
    count = rows.shape[0]
    ids = rows[:, 4, 0:1].astype(jnp.int32)
    lane = lax.broadcasted_iota(jnp.int32, (count, SPEAKERS), 1)
    one_hot = (lane == ids).astype(f32)

    def per_speaker(x):
        return lax.dot_general(
            one_hot, x, (((0,), (0,)), ((), ())), precision=highest, preferred_element_type=f32
        )

    sums = per_speaker(rows[:, 0, :])
    frames = per_speaker(jnp.full((count, BLOCK), float(BLOCK), f32))
    power[...] = sums / jnp.maximum(frames[:, 0:1], 1.0)
    two[...] = jnp.sum(rows[:, 1, :], axis=0, keepdims=True)
    gain[...] = jnp.sum(rows[:, 2, :], axis=0, keepdims=True)
    one[...] = jnp.sum(rows[:, 3, :], axis=0, keepdims=True)


def kernel_pieces(pieces):
    if len(pieces) == PIECES:
        return pieces
    ordered = from_pieces(jnp.concatenate(pieces, axis=0), 0)
    size = ordered.shape[0] // PIECES
    split = [ordered[b * size : (b + 1) * size] for b in range(PIECES)]
    return [split[(j % 4) * 2 + j // 4] for j in range(PIECES)]


def far_order(x):
    count = far_count()
    far = lax.axis_index(FAR)
    size = x.shape[0] // count
    return jnp.concatenate(
        [lax.dynamic_slice_in_dim(x, (far ^ k) * size, size, 0) for k in range(count)], axis=0
    )


def line_pieces(pieces):
    if len(pieces) == LINE:
        return pieces
    return jnp.split(far_order(jnp.concatenate(pieces, axis=0)), LINE, axis=0)


def slice_weights(sources, halves=1):
    rows = sources[0][0].shape[0]
    parts = []
    for x, count in sources:
        width = x.shape[1] // (4 * count * halves)
        parts.append(
            x.reshape(rows, count, 4, halves, width)
            .transpose(2, 0, 3, 1, 4)
            .reshape(4, rows, halves, count * width)
        )
    joined = jnp.concatenate(parts, axis=3)
    return joined.reshape(4, rows, halves * joined.shape[3])


def quarter_columns(x):
    near, pair = lax.axis_index(NEAR), lax.axis_index(PAIR)
    both = (NEAR, PAIR)
    across = [(i, 3 - i) for i in range(4)]

    def part(i, k):
        rows = lax.dynamic_index_in_dim(x, pair ^ i, 0, keepdims=False)
        return lax.dynamic_slice_in_dim(rows, (near ^ k) * (rows.shape[1] // 2), rows.shape[1] // 2, 1)

    came = {
        (0, 0): part(0, 0),
        (0, 1): swap(part(0, 1), NEAR),
        (1, 0): swap(part(1, 0), PAIR),
        (1, 1): lax.ppermute(part(1, 1), both, across),
    }
    by_near = [
        (jnp.where(near == 0, came[i, 0], came[i, 1]), jnp.where(near == 0, came[i, 1], came[i, 0]))
        for i in range(2)
    ]
    out = []
    for k in range(2):
        out.append(jnp.where(pair == 0, by_near[0][k], by_near[1][k]))
        out.append(jnp.where(pair == 0, by_near[1][k], by_near[0][k]))
    return jnp.concatenate(out, axis=0)


def sum_wide(own, other, outs):
    if far_count() != LINE:
        return sum_wide_long(own, other, outs), []
    whole = [(own[0].shape[1], bf16)]
    near = [swap(x, NEAR) for x in other]
    third = merge([own[3], near[3]], whole)
    halfway = merge([own[2], near[2], swap_far(third[0], 1)], whole)[0]
    first = merge([own[1], near[1]], whole, third)[0]
    return merge([own[0], near[0], swap_far(first, 1), swap_far(halfway, 2)], outs), third


def sum_wide_long(own, other, outs):
    count = far_count()
    ordered = [(own + other)[(b % 2) * 4 + b // 2] for b in range(PIECES)]
    pieces = to_pieces(jnp.concatenate([x.astype(f32) for x in ordered], axis=0), 0)
    size = pieces.shape[0] // (2 * count)
    parts = {}
    for i in range(2):
        for k in range(count):
            at = (i * count + k) * size
            parts[i, k] = pieces[at : at + size]
    total = scatter_parts(parts)
    at = 0
    result = []
    for width, dtype in outs:
        result.append(total[:, at : at + width].astype(dtype))
        at += width
    return result


def split_rows(terms, after):
    rows, width = terms[0].shape
    if rows % 32 != 0:
        near = lax.axis_index(NEAR)
        total = sum(x.astype(f32) for x in terms).reshape(2, rows // 2, width)
        return (
            lax.dynamic_index_in_dim(total, near, 0, keepdims=False),
            lax.dynamic_index_in_dim(total, 1 - near, 0, keepdims=False).astype(bf16),
        )
    return call(
        lambda *refs: split_rows_kernel(refs[: len(terms)], refs[len(terms) :]),
        "merge",
        [((rows // 2, width), f32), ((rows // 2, width), bf16)],
        terms,
        after=after,
    )


def sum_line(parts):
    count = far_count()
    pieces = jnp.split(far_order(jnp.concatenate(parts, axis=0).astype(f32)), count, axis=0)
    for j in range(count - 1, 0, -1):
        low = j & -j
        pieces[j ^ low] = pieces[j ^ low] + swap_far(pieces[j].astype(bf16), low).astype(f32)
    return pieces[0]


def body(
    frames,
    out_grad,
    qkv_weight,
    out_weight,
    gate_up_weight,
    down_weight_t,
    norm_gain_one,
    norm_gain_two,
    layer_scale_one,
    layer_scale_two,
    speaker,
    clip_bounds,
):
    streams, shard_len, width = frames.shape
    pair = lax.axis_index(PAIR)
    core = lax.axis_index(CORE)
    near = lax.axis_index(NEAR)
    shard = pair * 2 + core
    group = width // 4
    hidden = gate_up_weight.shape[1] // 16
    head_size = width // HEADS
    tokens = 4 * shard_len

    slice_a = pair_columns(core_columns(slice_weights([(qkv_weight, 3), (out_weight, 1)])))
    slice_b = quarter_columns(core_columns(slice_weights([(gate_up_weight, 2), (down_weight_t, 1)], halves=2)))
    pieces_a = kernel_pieces(gather_rows(slice_a))
    line_b = gather_line(slice_b)
    pieces_b = line_pieces(line_b)

    bounds = clip_bounds.astype(jnp.int32)
    gain_one = norm_gain_one[None]
    gain_two = norm_gain_two[None]
    scale_one = layer_scale_one[None]
    scale_two = layer_scale_two[None]
    frames_here, grad_here = call(
        copy_kernel,
        "fence",
        [((shard_len, width), bf16)] * 2,
        [frames.reshape(shard_len, width), out_grad.reshape(shard_len, width)],
        after=[slice_a],
    )

    def spread(x):
        across = swap(x, PAIR)
        return x, swap(x, CORE), across, swap(across, CORE)

    frames_all = spread(frames_here)
    grad_all = (*spread(grad_here), *spread(swap(grad_here, NEAR)))

    block = shard ^ jnp.arange(4, dtype=jnp.int32)
    positions = (block[:, None] * shard_len + jnp.arange(shard_len, dtype=jnp.int32)[None]).reshape(-1)
    half_size = head_size // 2
    lane = jnp.arange(BLOCK, dtype=jnp.int32)
    inverse_freq = jnp.exp((lane % half_size).astype(f32) * (-math.log(10000.0) / half_size))
    angles = positions.astype(f32)[:, None] * inverse_freq[None, :]
    cosine = jnp.cos(angles)
    sine = jnp.where(lane % head_size < half_size, -1.0, 1.0)[None, :] * jnp.sin(angles)

    (out_own,) = call(
        out_kernel,
        "out",
        [((width, group), bf16)],
        pieces_a,
        [pltpu.SemaphoreType.DMA((PIECES,))],
        anywhere=range(PIECES),
    )
    normed_one, qkv, stat, att, att_to_core, att_to_pair = call(
        attend_kernel,
        "attend",
        [
            ((tokens, width), bf16),
            ((tokens, 3 * group), bf16),
            ((tokens, BLOCK), f32),
            ((tokens, group), bf16),
            ((tokens, group), bf16),
            ((tokens, group), bf16),
        ],
        [bounds, *frames_all, *pieces_a, gain_one, cosine, sine],
        [pltpu.VMEM((width, 3 * group), bf16), pltpu.SemaphoreType.DMA((PIECES,))],
        smem=1,
        anywhere=range(5, 5 + PIECES),
        megabytes=52,
        after=[line_b[1], line_b[2], out_own],
    )
    att_pair = swap(att_to_pair, PAIR)
    att_core = swap(att_to_core, CORE)
    att_both = swap(att_pair, CORE)
    out_pair = swap(out_own, PAIR)
    outs = (out_own, swap(out_own, CORE), out_pair, swap(out_pair, CORE))

    normed_here, normed_even, attended, residual, branch_one = call(
        residual_kernel,
        "residual",
        [
            ((tokens, width), bf16),
            ((tokens // 2, width), bf16),
            ((tokens, width), bf16),
            ((shard_len, width), f32),
            ((shard_len, width), f32),
        ],
        [*frames_all, att, att_core, att_pair, att_both, *outs, scale_one, gain_two],
        [pltpu.VMEM((tokens, width), f32)],
        megabytes=52,
        after=[line_b[1], line_b[3], *grad_all],
    )

    near_even = swap(normed_even, NEAR)
    near_odd = swap(near_even, CORE)
    rows_b = width // LINE
    keep, send, keep_late, send_late, *grads_b = call(
        mlp_kernel,
        "mlp",
        [((tokens, width), bf16)] * 4 + [((rows_b, 3 * hidden), bf16)] * LINE,
        [normed_here, near_even, near_odd, *grad_all, *pieces_b, scale_two],
        [
            pltpu.VMEM((2 * tokens, width), bf16),
            pltpu.VMEM((2 * tokens, width), bf16),
            pltpu.VMEM((2 * tokens, hidden), bf16),
            pltpu.VMEM((2 * tokens, 2 * hidden), bf16),
            pltpu.VMEM((width, 3 * hidden), bf16),
            pltpu.SemaphoreType.DMA((LINE,)),
        ],
        anywhere=range(11, 11 + LINE),
        megabytes=52,
    )

    half_shape = ((2 * shard_len, width), bf16)
    own_shape = ((shard_len, width), bf16)

    got = swap(send, CORE)
    to_near = call(near_kernel, "onward", [half_shape], [keep, got])[0]
    got_near = swap(to_near, NEAR)
    got_late = swap(send_late, CORE)
    to_near_late = call(near_kernel, "onward", [half_shape], [keep_late, got_late], after=[to_near])[0]
    to_pair = call(pair_kernel, "onward", [own_shape], [keep, got, got_near], after=[to_near_late])[0]
    near_late = swap(to_near_late, NEAR)
    residual_grad, attn_grad, rows = call(
        middle_kernel,
        "middle",
        [((shard_len, width), f32), ((shard_len, width), bf16), ((8, width), f32)],
        [keep, got, got_near, swap(to_pair, PAIR), grad_here, residual, branch_one, scale_one, gain_two],
    )
    to_pair_late = call(
        pair_kernel, "onward", [own_shape], [keep_late, got_late, near_late], after=[attn_grad]
    )[0]
    met_late = (keep_late, got_late, near_late, swap(to_pair_late, PAIR))
    if far_count() == LINE:
        third_b, first_b = swap_far(grads_b[3], 1), swap_far(grads_b[1], 1)
        halfway_b = merge([grads_b[2], third_b], [(3 * hidden, bf16)], [attn_grad])[0]
        terms_b = [grads_b[0], first_b, swap_far(halfway_b, 2)]
    else:
        halfway_b = sum_line(grads_b)
        terms_b = [halfway_b]
    keep, send, *grads_a = call(
        attend_back_kernel,
        "attend_back",
        [((2 * shard_len, width), f32), ((2 * shard_len, width), bf16)]
        + [((BLOCK, 4 * group), bf16)] * PIECES,
        [bounds, *spread(attn_grad), qkv, stat, cosine, sine, *outs, *pieces_a, normed_one, attended],
        [
            pltpu.VMEM((tokens, 3 * group), bf16),
            pltpu.VMEM((width, 3 * group), bf16),
            pltpu.VMEM((tokens, width), bf16),
            pltpu.VMEM((tokens, group), bf16),
            pltpu.VMEM((tokens, tokens), bf16),
            pltpu.VMEM((tokens, tokens), bf16),
            pltpu.VMEM((4, group, group), bf16),
            pltpu.VMEM((tokens, width), bf16),
            pltpu.VMEM((tokens, width), bf16),
            pltpu.SemaphoreType.DMA((6 + PIECES,)),
        ],
        smem=1,
        anywhere=range(9, 15 + PIECES),
        megabytes=24,
        after=[to_pair_late, halfway_b],
    )
    own_a, other_a = grads_a[:4], grads_a[4:]
    got = swap(send, CORE)
    onward = call(onward_kernel, "onward", [((shard_len, width), bf16)], [keep, got])[0]
    output, early_spread = call(
        finish_kernel,
        "finish",
        [((shard_len, width), bf16), ((far_count() * 8, 5, width), f32)],
        [speaker.astype(jnp.int32), *met_late, grad_here, residual, rows, scale_two],
        smem=1,
        after=[onward],
    )
    (query_sum, key_sum, value_sum, out_sum), third_a = sum_wide(
        own_a, other_a, [(group, bf16)] * 3 + [(group, f32)]
    )
    kept_b, left_b = split_rows(terms_b, third_a)
    came_b = swap(left_b, NEAR)
    def everywhere(vectors):
        return lax.all_to_all(vectors, ALL, 0, 0, tiled=True)

    early = everywhere(early_spread)
    frames_grad, late_spread = call(
        last_kernel,
        "last",
        [((shard_len, width), bf16), ((far_count() * 8, 1, width), f32)],
        [keep, got, swap(onward, PAIR), frames_here, residual_grad, gain_one],
        after=(),
    )
    late = everywhere(late_spread)
    speaker_power, gain_two_grad, scale_one_grad, scale_two_grad = call(
        totals_kernel, "totals", [((SPEAKERS, width), f32)] + [((1, width), f32)] * 3, [early]
    )

    def near_order(kept, came):
        return jnp.concatenate(
            [jnp.where(near == 0, kept, came), jnp.where(near == 0, came, kept)], axis=1
        )

    kept_low = kept_b[:, : 2 * hidden].astype(bf16)
    gate_up_grad_out = place_gate_up(
        near_order(kept_low[:, :hidden], came_b[:, :hidden]),
        near_order(kept_low[:, hidden:], came_b[:, hidden : 2 * hidden]),
        pair,
        core,
    )
    down_grad = near_order(kept_b[:, 2 * hidden :], came_b[:, 2 * hidden :].astype(f32))
    qkv_grad_out = place_qkv(query_sum, key_sum, value_sum, pair, core)
    return (
        output.reshape(frames.shape),
        speaker_power,
        frames_grad.reshape(frames.shape),
        qkv_grad_out,
        out_sum,
        gate_up_grad_out,
        down_grad,
        jnp.sum(late[:, 0], axis=0),
        gain_two_grad[0],
        scale_one_grad[0],
        scale_two_grad[0],
    )


def place_gate_up(gate, up, pair, core):
    narrow = (PAIR, CORE)
    shard = pair * 2 + core
    first = jnp.where(shard == 1, up, gate)
    second = jnp.where(shard == 0, up, gate)
    second = jnp.where(shard == 2, up, second)
    got_one = lax.ppermute(first, narrow, [(1, 2), (2, 1)])
    got_two = lax.ppermute(second, narrow, [(0, 2), (1, 0), (2, 3), (3, 1)])
    left = jnp.where(shard == 0, gate, jnp.where(shard == 1, got_one, got_two))
    right = jnp.where(shard == 3, up, jnp.where(shard == 2, got_one, got_two))
    return jnp.concatenate([left, right], axis=1).astype(f32)


def place_qkv(query, key, value, pair, core):
    shard = pair * 2 + core
    to_core = jnp.where(
        shard == 0, key, jnp.where(shard == 1, query, jnp.where(shard == 2, value, key))
    )
    to_pair = jnp.where(pair == 0, value, query)
    stay = jnp.where(shard == 0, query, jnp.where(shard == 3, value, key))
    got_core = swap(to_core, CORE)
    got_pair = swap(to_pair, PAIR)
    left = jnp.where(core == 0, stay, got_pair)
    right = jnp.where(core == 0, got_pair, stay)
    return jnp.concatenate([left, got_core, right], axis=1).astype(f32)


def solution(mesh):
    wide = mesh.shape["wide"]
    split = Mesh(mesh.devices.reshape(wide // 2, 2, 2, 2), ALL)
    both = (FAR, NEAR)
    narrow = (PAIR, CORE)
    placed = (
        P(both, narrow, None),
        P(both, narrow, None),
        P(ALL, None),
        P(ALL, None),
        P(ALL, None),
        P(ALL, None),
        P(),
        P(),
        P(),
        P(),
        P(both),
        P(both, None),
    )
    return jax.shard_map(
        body,
        mesh=split,
        in_specs=placed,
        out_specs=(
            P(both, narrow, None),
            P(),
            P(both, narrow, None),
            P(both, narrow),
            P(both, narrow),
            P(both, narrow),
            P(both, narrow),
            P(),
            P(),
            P(),
            P(),
        ),
        check_vma=False,
    )
```

profile of v0, /device:TPU:0, one launch (start us, length us, event | category | flops | bytes accessed | tf_op | source)
XLA Modules:
  0.0 287.6 jit_solution(8965437163554727877)
XLA Ops:
  0.7 1.1 reshape.282
  5.5 2.6 collective-permute-start.1
  8.5 1.6 collective-permute-start.13
  10.0 1.4 collective-permute-start.14
  12.4 2.9 collective-permute-start.6
  15.2 1.6 collective-permute-start.5
  16.9 2.0 collective-permute-start.8
  18.9 1.7 collective-permute-done.14
  20.5 1.9 collective-permute-start.3
  22.7 4.5 %collective-permute-done.6.refs_2_.refs_7_.refs_15_ = bf16[128,1024]{1,0:T(8,128)(2,1)S(1)} collective-permute-done((bf16[128,1024]{1,0:T(8,128)(2,1)S(1)}, bf16[128,1024]{1,0:T(8,128)(2,1)S(1)}, u32[]{:S(2)}, u32[]{:S(2)}) %collective-permute-start.6) | collective-permute-done | bytes 262176 | tf_op jit(solution)/shard_map/ppermute | solution.py:72
  27.2 1.5 collective-permute-start.28
  30.2 1.5 collective-permute-start.16
  31.7 2.0 collective-permute-start.17
  34.9 1.5 collective-permute-start.9
  36.4 18.4 %collective-permute-done.7.refs_3_.refs_8_.refs_16_ = bf16[128,1024]{1,0:T(8,128)(2,1)S(1)} collective-permute-done((bf16[128,1024]{1,0:T(8,128)(2,1)S(1)}, bf16[128,1024]{1,0:T(8,128)(2,1)S(1)}, u32[]{:S(2)}, u32[]{:S(2)}) %collective-permute-start.7) | collective-permute-done | bytes 262176 | tf_op jit(solution)/shard_map/ppermute | solution.py:72
  55.3 1.5 collective-permute-start.26
  57.0 4.2 %collective-permute-done.11.refs_7_.refs_12_.refs_20_ = bf16[128,1024]{1,0:T(8,128)(2,1)S(1)} collective-permute-done((bf16[128,1024]{1,0:T(8,128)(2,1)S(1)}, bf16[128,1024]{1,0:T(8,128)(2,1)S(1)}, u32[]{:S(2)}, u32[]{:S(2)}) %collective-permute-start.11) | collective-permute-done | bytes 262176 | tf_op jit(solution)/shard_map/ppermute | solution.py:26
  61.9 1.5 collective-permute-start.22
  64.1 5.3 %collective-permute-done.16.refs_16_.refs_14_.refs_9_ = bf16[256,1536]{1,0:T(8,128)(2,1)} collective-permute-done((bf16[256,1536]{1,0:T(8,128)(2,1)}, bf16[256,1536]{1,0:T(8,128)(2,1)}, u32[]{:S(2)}, u32[]{:S(2)}) %collective-permute-start.16) | collective-permute-done | bytes 786464 | tf_op jit(solution)/shard_map/ppermute | solution.py:72
  69.3 3.3 %collective-permute-start.24 = (bf16[256,1536]{1,0:T(8,128)(2,1)}, bf16[256,1536]{1,0:T(8,128)(2,1)S(1)}, u32[]{:S(2)}, u32[]{:S(2)}) collective-permute-start(bf16[256,1536]{1,0:T(8,128)(2,1)} %collective-permute-done.17.refs_17_.refs_10_), channel_id=1, source_target_pairs={{0,8},{8,0},{16,24},{24,16},{1,9},{9,1},{17,25},{25,17},{2,10},{10... | collective-permute-start | bytes 2359304 | tf_op jit(solution)/shard_map/ppermute | solution.py:72
  72.7 2.1 fusion
  74.8 10.1 %attend.1 = (bf16[512,1024]{1,0:T(8,128)(2,1)}, bf16[512,768]{1,0:T(8,128)(2,1)}, f32[512,128]{1,0:T(8,128)S(1)}, bf16[512,256]{1,0:T(8,128)(2,1)S(1)}, bf16[512...) custom-call(s32[1,2]{1,0:T(1,128)S(1)} %copy-done.76, bf16[128,1024]{1,0:T(8,128)(2,1)S(1)} %get-tuple-element.59.refs_1_.refs_0_.frames, ...), custom_call_target="tpu_custom_call" | custom-call | flops 900000000 | tf_op jit(solution)/shard_map/attend/pallas_call | solution.py:142
  85.5 1.5 collective-permute-start.19
  87.5 6.3 %collective-permute-done.19.refs_6_ = bf16[512,256]{1,0:T(8,128)(2,1)S(1)} collective-permute-done((bf16[512,256]{1,0:T(8,128)(2,1)S(1)}, bf16[512,256]{1,0:T(8,128)(2,1)S(1)}, u32[]{:S(2)}, u32[]{:S(2)}) %collective-permute-start.19) | collective-permute-done | bytes 262176 | tf_op jit(solution)/shard_map/ppermute | solution.py:26
  93.8 1.5 collective-permute-done.20.refs_7_
  97.5 5.7 %residual.1 = (bf16[512,1024]{1,0:T(8,128)(2,1)}, bf16[256,1024]{1,0:T(8,128)(2,1)}, bf16[512,1024]{1,0:T(8,128)(2,1)}, f32[128,1024]{1,0:T(8,128)}, f32[128,1024]{1,0:T(8,128)}) custom-call(bf16[128,1024]{1,0:T(8,128)(2,1)S(1)} %get-tuple-element.59.refs_1_.refs_0_.frames, bf16[128,1024]{1,0:T(8,128)(2,1)S(1)} %copy-done.53, ...), custom_call_target="tpu_custom_call" | custom-call | flops 300000000 | tf_op jit(solution)/shard_map/residual/pallas_call | solution.py:142
  103.8 13.6 %collective-permute-done.32.near_even = bf16[256,1024]{1,0:T(8,128)(2,1)S(1)} collective-permute-done((bf16[256,1024]{1,0:T(8,128)(2,1)}, bf16[256,1024]{1,0:T(8,128)(2,1)S(1)}, u32[]{:S(2)}, u32[]{:S(2)}) %collective-permute-start.32) | collective-permute-done | bytes 524320 | tf_op jit(solution)/shard_map/ppermute | solution.py:26
  117.4 1.9 collective-permute-done.33.near_odd
  123.0 28.5 %mlp.1 = (bf16[512,1024]{1,0:T(8,128)(2,1)}, bf16[512,1024]{1,0:T(8,128)(2,1)}, bf16[512,1024]{1,0:T(8,128)(2,1)}, bf16[512,1024]{1,0:T(8,128)(2,1)}, bf16[256,1...) custom-call(bf16[512,1024]{1,0:T(8,128)(2,1)} %get-tuple-element.64.normed_h, ...), custom_call_target="tpu_custom_call" | custom-call | flops 1100000000 | tf_op jit(solution)/shard_map/mlp/pallas_call | solution.py:142
  152.0 2.4 collective-permute-done.35.got.refs_1_
  154.4 1.2 copy-done.1
  157.2 12.5 %collective-permute-done.37.refs_2_.got_near = bf16[256,1024]{1,0:T(8,128)(2,1)S(1)} collective-permute-done((bf16[256,1024]{1,0:T(8,128)(2,1)S(1)}, bf16[256,1024]{1,0:T(8,128)(2,1)S(1)}, u32[]{:S(2)}, u32[]{:S(2)}) %collective-permute-start.37) | collective-permute-done | bytes 524320 | tf_op jit(solution)/shard_map/ppermute | solution.py:26
  169.9 1.6 collective-permute-start.38
  172.0 5.5 %collective-permute-done.38.got_pair = bf16[128,1024]{1,0:T(8,128)(2,1)S(1)} collective-permute-done((bf16[128,1024]{1,0:T(8,128)(2,1)S(1)}, bf16[128,1024]{1,0:T(8,128)(2,1)S(1)}, u32[]{:S(2)}, u32[]{:S(2)}) %collective-permute-start.38) | collective-permute-done | bytes 262176 | tf_op jit(solution)/shard_map/ppermute | solution.py:26
  179.0 1.5 collective-permute-start.41
  180.9 2.2 collective-permute-start.56
  183.1 2.5 collective-permute-done.41.refs_3_
  187.3 13.1 %attend_back.1 = (f32[256,1024]{1,0:T(8,128)S(1)}, bf16[256,1024]{1,0:T(8,128)(2,1)}, bf16[128,1024]{1,0:T(8,128)(2,1)S(1)}, bf16[128,1024]{1,0:T(8,128)(2,1)S(1...) custom-call(s32[1,2]{1,0:T(1,128)S(1)} %copy-done.76, ...), custom_call_target="tpu_custom_call" | custom-call | flops 1100000000 | tf_op jit(solution)/shard_map/attend_back/pallas_call | solution.py:142
  201.0 1.5 collective-permute-start.47
  202.5 7.1 %collective-permute-done.48.refs_1_ = bf16[128,1024]{1,0:T(8,128)(2,1)S(1)} collective-permute-done((bf16[128,1024]{1,0:T(8,128)(2,1)S(1)}, bf16[128,1024]{1,0:T(8,128)(2,1)S(1)}, u32[]{:S(2)}, u32[]{:S(2)}) %collective-permute-start.48) | collective-permute-done | bytes 262176 | tf_op jit(solution)/shard_map/ppermute | solution.py:26
  210.4 4.5 %collective-permute-done.55.refs_1_ = bf16[256,1536]{1,0:T(8,128)(2,1)S(1)} collective-permute-done((bf16[256,1536]{1,0:T(8,128)(2,1)S(1)}, bf16[256,1536]{1,0:T(8,128)(2,1)S(1)}, u32[]{:S(2)}, u32[]{:S(2)}) %collective-permute-start.55) | collective-permute-done | bytes 786464 | tf_op jit(solution)/shard_map/ppermute | solution.py:72
  217.8 1.5 collective-permute-start.50
  220.0 1.9 collective-permute-start.51
  222.7 1.2 convert.3
  225.2 1.1 onward.9.refs_9_
  226.4 2.4 finish.1
  228.8 5.9 %collective-permute-done.50.refs_1_ = bf16[128,1024]{1,0:T(8,128)(2,1)} collective-permute-done((bf16[128,1024]{1,0:T(8,128)(2,1)}, bf16[128,1024]{1,0:T(8,128)(2,1)}, u32[]{:S(2)}, u32[]{:S(2)}) %collective-permute-start.50) | collective-permute-done | bytes 262176 | tf_op jit(solution)/shard_map/ppermute | solution.py:26
  235.3 1.1 merge.9
  237.0 1.0 broadcast_select_fusion.14
  238.9 1.4 collective-permute-start.58
  241.1 1.2 collective-permute-start.59
  242.4 2.2 last.1
  244.6 4.0 %all-to-all-start.1 = ((f32[32,1,1024]{2,1,0:T(1,128)}), f32[32,1,1024]{2,1,0:T(1,128)S(1)}, u32[]{:S(2)}, u32[]{:S(2)}) async-start(f32[32,1,1024]{2,1,0:T(1,128)} %get-tuple-element.103), calls=%async_computation.1 | async-start | bytes 262144 | tf_op jit(solution)/shard_map/all_to_all | solution.py:907
  248.6 1.0 convert_select_fusion.1
  249.7 1.7 merge.10
  251.4 5.4 %all-to-all-done.1 = f32[32,1,1024]{2,1,0:T(1,128)S(1)} async-done(((f32[32,1,1024]{2,1,0:T(1,128)}), f32[32,1,1024]{2,1,0:T(1,128)S(1)}, u32[]{:S(2)}, u32[]{:S(2)}) %all-to-all-start.1) | async-done | bytes 131104 | tf_op jit(solution)/shard_map/all_to_all | solution.py:907
  256.8 2.6 all-to-all-start
  259.5 1.7 collective-permute-start.53
  262.1 7.6 %collective-permute-done.53 = bf16[128,256]{1,0:T(8,128)(2,1)S(1)} collective-permute-done((bf16[128,256]{1,0:T(8,128)(2,1)S(1)}, bf16[128,256]{1,0:T(8,128)(2,1)S(1)}, u32[]{:S(2)}, u32[]{:S(2)}) %collective-permute-start.53) | collective-permute-done | bytes 65568 | tf_op jit(solution)/shard_map/ppermute | solution.py:26
  269.8 1.2 collective-permute-done.54
  271.8 1.2 select_select_fusion.2
  273.0 1.1 maximum_convert_fusion
  274.7 11.0 %all-to-all-done.rows = f32[32,5,1024]{2,1,0:T(8,128)S(1)} async-done(((f32[32,5,1024]{2,1,0:T(8,128)}), f32[32,5,1024]{2,1,0:T(8,128)S(1)}, u32[]{:S(2)}, u32[]{:S(2)}) %all-to-all-start) | async-done | bytes 655392 | tf_op jit(solution)/shard_map/all_to_all | solution.py:907
  285.7 1.7 totals.1
  (302 shorter events, 34.9 us)
Async XLA Ops:
  2.3 3.1 %collective-permute-start = (bf16[2,32,1024]{2,1,0:T(8,128)(2,1)S(1)}, bf16[2,32,1024]{2,1,0:T(8,128)(2,1)S(1)}, u32[]{:S(2)}, u32[]{:S(2)}) collective-permute-start(bf16[2,32,1024]{2,1,0:T(8,128)(2,1)S(1)} %pad_maximum_fusion.9), channel_id=1, source_target_pairs={{0,1},{1,0},{2,3},{3,2},{4,5},{5,4},{6,7},{7,6},{8,9},{9,8},{10,11... | collective-permute-start | bytes 393224 | tf_op jit(solution)/shard_map/ppermute | solution.py:26
  4.8 3.3 %collective-permute-start.12 = (bf16[2,32,3072]{2,1,0:T(8,128)(2,1)S(1)}, bf16[2,32,3072]{2,1,0:T(8,128)(2,1)S(1)}, u32[]{:S(2)}, u32[]{:S(2)}) collective-permute-start(bf16[2,32,3072]{2,1,0:T(8,128)(2,1)S(1)} %pad_maximum_fusion.2), channel_id=1, source_target_pairs={{0,1},{1,0},{2,3},{3,2},{4,5},{5,4},{6,7},{7,6},{8,9},{9,8},{10,11... | collective-permute-start | bytes 1179656 | tf_op jit(solution)/shard_map/ppermute | solution.py:26
  5.5 6.8 %collective-permute-start.1 = (bf16[64,1024]{1,0:T(8,128)(2,1)S(1)}, bf16[64,1024]{1,0:T(8,128)(2,1)S(1)}, u32[]{:S(2)}, u32[]{:S(2)}) collective-permute-start(bf16[64,1024]{1,0:T(8,128)(2,1)S(1)} %select_bitcast_fusion.4), channel_id=1, source_target_pairs={{0,2},{2,0},{1,3},{3,1},{4,6},{6,4},{5,7},{7,5},{8,10},{10,8},{9,1... | collective-permute-start | bytes 393224 | tf_op jit(solution)/shard_map/ppermute | solution.py:26
  8.5 8.4 %collective-permute-start.13 = (bf16[64,1536]{1,0:T(8,128)(2,1)S(1)}, bf16[64,1536]{1,0:T(8,128)(2,1)S(1)}, u32[]{:S(2)}, u32[]{:S(2)}) collective-permute-start(bf16[64,1536]{1,0:T(8,128)(2,1)S(1)} %get-tuple-element.125), channel_id=1, source_target_pairs={{0,4},{4,0},{1,5},{5,1},{2,6},{6,2},{3,7},{7,3},{8,12},{12,8},{9,1... | collective-permute-start | bytes 589832 | tf_op jit(solution)/shard_map/ppermute | solution.py:26
  10.0 10.5 %collective-permute-start.14 = (bf16[64,1536]{1,0:T(8,128)(2,1)S(1)}, bf16[64,1536]{1,0:T(8,128)(2,1)S(1)}, u32[]{:S(2)}, u32[]{:S(2)}) collective-permute-start(bf16[64,1536]{1,0:T(8,128)(2,1)S(1)} %get-tuple-element.126), channel_id=1, source_target_pairs={{0,2},{2,0},{1,3},{3,1},{4,6},{6,4},{5,7},{7,5},{8,10},{10,8},{9,1... | collective-permute-start | bytes 589832 | tf_op jit(solution)/shard_map/ppermute | solution.py:26
  11.5 11.0 %collective-permute-start.15 = (bf16[64,1536]{1,0:T(8,128)(2,1)S(1)}, bf16[64,1536]{1,0:T(8,128)(2,1)S(1)}, u32[]{:S(2)}, u32[]{:S(2)}) collective-permute-start(bf16[64,1536]{1,0:T(8,128)(2,1)S(1)} %get-tuple-element.124), channel_id=1, source_target_pairs={{0,6},{2,4},{4,2},{6,0},{1,7},{3,5},{5,3},{7,1},{8,14},{10,12},{12... | collective-permute-start | bytes 589832 | tf_op jit(solution)/shard_map/ppermute | solution.py:643
  12.4 48.8 %copy-start.5 = (bf16[128,1024]{1,0:T(8,128)(2,1)}, bf16[128,1024]{1,0:T(8,128)(2,1)S(1)}, u32[]{:S(2)}) copy-start(bf16[128,1024]{1,0:T(8,128)(2,1)S(1)} %pad_maximum_fusion.3.refs_2_.refs_0_.refs_5_.refs_13_) | copy-start | bytes 786436
  12.4 14.8 %collective-permute-start.6 = (bf16[128,1024]{1,0:T(8,128)(2,1)S(1)}, bf16[128,1024]{1,0:T(8,128)(2,1)S(1)}, u32[]{:S(2)}, u32[]{:S(2)}) collective-permute-start(bf16[128,1024]{1,0:T(8,128)(2,1)S(1)} %pad_maximum_fusion.3.refs_2_.refs_0_.refs_5_.refs_13_), channel_id=1, source_target_pairs={{0,16},{8,24},{16,0},{24,8},{1,17},{9,25},{17,1},{25,9},{2,18},{10... | collective-permute-start | bytes 786440 | tf_op jit(solution)/shard_map/ppermute | solution.py:72
  15.2 13.4 %collective-permute-start.5 = (bf16[128,1024]{1,0:T(8,128)(2,1)S(1)}, bf16[128,1024]{1,0:T(8,128)(2,1)S(1)}, u32[]{:S(2)}, u32[]{:S(2)}) collective-permute-start(bf16[128,1024]{1,0:T(8,128)(2,1)S(1)} %pad_maximum_fusion.3.refs_2_.refs_0_.refs_5_.refs_13_), channel_id=1, source_target_pairs={{0,8},{8,0},{16,24},{24,16},{1,9},{9,1},{17,25},{25,17},{2,10},{10... | collective-permute-start | bytes 786440 | tf_op jit(solution)/shard_map/ppermute | solution.py:72
  16.9 78.5 %copy-start.9 = (bf16[128,1024]{1,0:T(8,128)(2,1)}, bf16[128,1024]{1,0:T(8,128)(2,1)S(1)}, u32[]{:S(2)}) copy-start(bf16[128,1024]{1,0:T(8,128)(2,1)S(1)} %get-tuple-element.59.refs_1_.refs_0_.frames) | copy-start | bytes 786436
  16.9 13.3 %collective-permute-start.8 = (bf16[128,1024]{1,0:T(8,128)(2,1)S(1)}, bf16[128,1024]{1,0:T(8,128)(2,1)S(1)}, u32[]{:S(2)}, u32[]{:S(2)}) collective-permute-start(bf16[128,1024]{1,0:T(8,128)(2,1)S(1)} %pad_maximum_fusion.3.refs_2_.refs_0_.refs_5_.refs_13_), channel_id=1, source_target_pairs={{0,4},{4,0},{1,5},{5,1},{2,6},{6,2},{3,7},{7,3},{8,12},{12,8},{9,1... | collective-permute-start | bytes 786440 | tf_op jit(solution)/shard_map/ppermute | solution.py:26
  20.5 11.1 %collective-permute-start.3 = (bf16[128,1024]{1,0:T(8,128)(2,1)S(1)}, bf16[128,1024]{1,0:T(8,128)(2,1)S(1)}, u32[]{:S(2)}, u32[]{:S(2)}) collective-permute-start(bf16[128,1024]{1,0:T(8,128)(2,1)S(1)} %get-tuple-element.59.refs_1_.refs_0_.frames), channel_id=1, source_target_pairs={{0,2},{2,0},{1,3},{3,1},{4,6},{6,4},{5,7},{7,5},{8,10},{10,8},{9,1... | collective-permute-start | bytes 786440 | tf_op jit(solution)/shard_map/ppermute | solution.py:26
  22.4 11.2 %collective-permute-start.2 = (bf16[128,1024]{1,0:T(8,128)(2,1)S(1)}, bf16[128,1024]{1,0:T(8,128)(2,1)S(1)}, u32[]{:S(2)}, u32[]{:S(2)}) collective-permute-start(bf16[128,1024]{1,0:T(8,128)(2,1)S(1)} %get-tuple-element.59.refs_1_.refs_0_.frames), channel_id=1, source_target_pairs={{0,1},{1,0},{2,3},{3,2},{4,5},{5,4},{6,7},{7,6},{8,9},{9,8},{10,11... | collective-permute-start | bytes 786440 | tf_op jit(solution)/shard_map/ppermute | solution.py:26
  27.2 7.8 %collective-permute-start.28 = (bf16[128,1024]{1,0:T(8,128)(2,1)S(1)}, bf16[128,1024]{1,0:T(8,128)(2,1)S(1)}, u32[]{:S(2)}, u32[]{:S(2)}) collective-permute-start(bf16[128,1024]{1,0:T(8,128)(2,1)S(1)} %get-tuple-element.63.refs_16_.refs_0_.own_grad.refs_5_), channel_id=1, source_target_pairs={{0,4},{4,0},{1,5},{5,1},{2,6},{6,2},{3,7},{7,3},{8,12},{12,8},{9,1... | collective-permute-start | bytes 786440 | tf_op jit(solution)/shard_map/ppermute | solution.py:26
  28.7 26.1 %collective-permute-start.7 = (bf16[128,1024]{1,0:T(8,128)(2,1)S(1)}, bf16[128,1024]{1,0:T(8,128)(2,1)S(1)}, u32[]{:S(2)}, u32[]{:S(2)}) collective-permute-start(bf16[128,1024]{1,0:T(8,128)(2,1)S(1)} %collective-permute-done.6.refs_2_.refs_7_.refs_15_), channel_id=1, source_target_pairs={{0,8},{8,0},{16,24},{24,16},{1,9},{9,1},{17,25},{25,17},{2,10},{10... | collective-permute-start | bytes 786440 | tf_op jit(solution)/shard_map/ppermute | solution.py:72
  30.2 39.1 %collective-permute-start.16 = (bf16[256,1536]{1,0:T(8,128)(2,1)}, bf16[256,1536]{1,0:T(8,128)(2,1)}, u32[]{:S(2)}, u32[]{:S(2)}) collective-permute-start(bf16[256,1536]{1,0:T(8,128)(2,1)} %pad_maximum_fusion.refs_8_), channel_id=1, source_target_pairs={{0,8},{8,0},{16,24},{24,16},{1,9},{9,1},{17,25},{25,17},{2,10},{10... | collective-permute-start | bytes 2359304 | tf_op jit(solution)/shard_map/ppermute | solution.py:72
  31.7 37.6 %collective-permute-start.17 = (bf16[256,1536]{1,0:T(8,128)(2,1)}, bf16[256,1536]{1,0:T(8,128)(2,1)}, u32[]{:S(2)}, u32[]{:S(2)}) collective-permute-start(bf16[256,1536]{1,0:T(8,128)(2,1)} %pad_maximum_fusion.refs_8_), channel_id=1, source_target_pairs={{0,16},{8,24},{16,0},{24,8},{1,17},{9,25},{17,1},{25,9},{2,18},{10... | collective-permute-start | bytes 2359304 | tf_op jit(solution)/shard_map/ppermute | solution.py:72
  34.4 20.9 %collective-permute-start.10 = (bf16[128,1024]{1,0:T(8,128)(2,1)S(1)}, bf16[128,1024]{1,0:T(8,128)(2,1)S(1)}, u32[]{:S(2)}, u32[]{:S(2)}) collective-permute-start(bf16[128,1024]{1,0:T(8,128)(2,1)S(1)} %collective-permute-done.6.refs_2_.refs_7_.refs_15_), channel_id=1, source_target_pairs={{0,4},{4,0},{1,5},{5,1},{2,6},{6,2},{3,7},{7,3},{8,12},{12,8},{9,1... | collective-permute-start | bytes 786440 | tf_op jit(solution)/shard_map/ppermute | solution.py:26
  34.9 21.9 %collective-permute-start.9 = (bf16[128,1024]{1,0:T(8,128)(2,1)S(1)}, bf16[128,1024]{1,0:T(8,128)(2,1)S(1)}, u32[]{:S(2)}, u32[]{:S(2)}) collective-permute-start(bf16[128,1024]{1,0:T(8,128)(2,1)S(1)} %collective-permute-done.5.refs_1_.refs_6_.refs_14_), channel_id=1, source_target_pairs={{0,4},{4,0},{1,5},{5,1},{2,6},{6,2},{3,7},{7,3},{8,12},{12,8},{9,1... | collective-permute-start | bytes 786440 | tf_op jit(solution)/shard_map/ppermute | solution.py:26
  54.8 6.4 %collective-permute-start.11 = (bf16[128,1024]{1,0:T(8,128)(2,1)S(1)}, bf16[128,1024]{1,0:T(8,128)(2,1)S(1)}, u32[]{:S(2)}, u32[]{:S(2)}) collective-permute-start(bf16[128,1024]{1,0:T(8,128)(2,1)S(1)} %collective-permute-done.7.refs_3_.refs_8_.refs_16_), channel_id=1, source_target_pairs={{0,4},{4,0},{1,5},{5,1},{2,6},{6,2},{3,7},{7,3},{8,12},{12,8},{9,1... | collective-permute-start | bytes 786440 | tf_op jit(solution)/shard_map/ppermute | solution.py:26
  55.3 6.5 %collective-permute-start.26 = (bf16[128,1024]{1,0:T(8,128)(2,1)S(1)}, bf16[128,1024]{1,0:T(8,128)(2,1)S(1)}, u32[]{:S(2)}, u32[]{:S(2)}) collective-permute-start(bf16[128,1024]{1,0:T(8,128)(2,1)S(1)} %get-tuple-element.63.refs_16_.refs_0_.own_grad.refs_5_), channel_id=1, source_target_pairs={{0,2},{2,0},{1,3},{3,1},{4,6},{6,4},{5,7},{7,5},{8,10},{10,8},{9,1... | collective-permute-start | bytes 786440 | tf_op jit(solution)/shard_map/ppermute | solution.py:26
  56.9 6.6 %collective-permute-start.25 = (bf16[128,1024]{1,0:T(8,128)(2,1)S(1)}, bf16[128,1024]{1,0:T(8,128)(2,1)S(1)}, u32[]{:S(2)}, u32[]{:S(2)}) collective-permute-start(bf16[128,1024]{1,0:T(8,128)(2,1)S(1)} %get-tuple-element.63.refs_16_.refs_0_.own_grad.refs_5_), channel_id=1, source_target_pairs={{0,1},{1,0},{2,3},{3,2},{4,5},{5,4},{6,7},{7,6},{8,9},{9,8},{10,11... | collective-permute-start | bytes 786440 | tf_op jit(solution)/shard_map/ppermute | solution.py:26
  61.2 2.8 collective-permute-start.4
  61.9 25.2 %collective-permute-start.22 = (bf16[1024,256]{1,0:T(8,128)(2,1)S(1)}, bf16[1024,256]{1,0:T(8,128)(2,1)S(1)}, u32[]{:S(2)}, u32[]{:S(2)}) collective-permute-start(bf16[1024,256]{1,0:T(8,128)(2,1)S(1)} %out.1.refs_18_.refs_8_.refs_9_), channel_id=1, source_target_pairs={{0,2},{2,0},{1,3},{3,1},{4,6},{6,4},{5,7},{7,5},{8,10},{10,8},{9,1... | collective-permute-start | bytes 1572872 | tf_op jit(solution)/shard_map/ppermute | solution.py:26
  63.5 21.4 %collective-permute-start.30 = (bf16[128,1024]{1,0:T(8,128)(2,1)S(1)}, bf16[128,1024]{1,0:T(8,128)(2,1)S(1)}, u32[]{:S(2)}, u32[]{:S(2)}) collective-permute-start(bf16[128,1024]{1,0:T(8,128)(2,1)S(1)} %collective-permute-done.28.refs_20_.refs_4_), channel_id=1, source_target_pairs={{0,2},{2,0},{1,3},{3,1},{4,6},{6,4},{5,7},{7,5},{8,10},{10,8},{9,1... | collective-permute-start | bytes 786440 | tf_op jit(solution)/shard_map/ppermute | solution.py:26
  64.0 21.5 %collective-permute-start.29 = (bf16[128,1024]{1,0:T(8,128)(2,1)S(1)}, bf16[128,1024]{1,0:T(8,128)(2,1)S(1)}, u32[]{:S(2)}, u32[]{:S(2)}) collective-permute-start(bf16[128,1024]{1,0:T(8,128)(2,1)S(1)} %collective-permute-done.28.refs_20_.refs_4_), channel_id=1, source_target_pairs={{0,1},{1,0},{2,3},{3,2},{4,5},{5,4},{6,7},{7,6},{8,9},{9,8},{10,11... | collective-permute-start | bytes 786440 | tf_op jit(solution)/shard_map/ppermute | solution.py:26
  69.3 15.7 %collective-permute-start.27 = (bf16[128,1024]{1,0:T(8,128)(2,1)S(1)}, bf16[128,1024]{1,0:T(8,128)(2,1)S(1)}, u32[]{:S(2)}, u32[]{:S(2)}) collective-permute-start(bf16[128,1024]{1,0:T(8,128)(2,1)S(1)} %collective-permute-done.26.refs_18_.refs_2_), channel_id=1, source_target_pairs={{0,1},{1,0},{2,3},{3,2},{4,5},{5,4},{6,7},{7,6},{8,9},{9,8},{10,11... | collective-permute-start | bytes 786440 | tf_op jit(solution)/shard_map/ppermute | solution.py:26
  69.3 26.0 %collective-permute-start.24 = (bf16[256,1536]{1,0:T(8,128)(2,1)}, bf16[256,1536]{1,0:T(8,128)(2,1)S(1)}, u32[]{:S(2)}, u32[]{:S(2)}) collective-permute-start(bf16[256,1536]{1,0:T(8,128)(2,1)} %collective-permute-done.17.refs_17_.refs_10_), channel_id=1, source_target_pairs={{0,8},{8,0},{16,24},{24,16},{1,9},{9,1},{17,25},{25,17},{2,10},{10... | collective-permute-start | bytes 2359304 | tf_op jit(solution)/shard_map/ppermute | solution.py:72
  84.9 2.1 collective-permute-start.31
  85.0 8.8 %collective-permute-start.21 = (bf16[1024,256]{1,0:T(8,128)(2,1)}, bf16[1024,256]{1,0:T(8,128)(2,1)S(1)}, u32[]{:S(2)}, u32[]{:S(2)}) collective-permute-start(bf16[1024,256]{1,0:T(8,128)(2,1)} %copy-done.3), channel_id=1, source_target_pairs={{0,1},{1,0},{2,3},{3,2},{4,5},{5,4},{6,7},{7,6},{8,9},{9,8},{10,11... | collective-permute-start | bytes 1572872 | tf_op jit(solution)/shard_map/ppermute | solution.py:26
  85.5 8.3 %collective-permute-start.19 = (bf16[512,256]{1,0:T(8,128)(2,1)S(1)}, bf16[512,256]{1,0:T(8,128)(2,1)S(1)}, u32[]{:S(2)}, u32[]{:S(2)}) collective-permute-start(bf16[512,256]{1,0:T(8,128)(2,1)S(1)} %get-tuple-element.62), channel_id=1, source_target_pairs={{0,2},{2,0},{1,3},{3,1},{4,6},{6,4},{5,7},{7,5},{8,10},{10,8},{9,1... | collective-permute-start | bytes 786440 | tf_op jit(solution)/shard_map/ppermute | solution.py:26
  87.0 8.3 %collective-permute-start.23 = (bf16[1024,256]{1,0:T(8,128)(2,1)S(1)}, bf16[1024,256]{1,0:T(8,128)(2,1)S(1)}, u32[]{:S(2)}, u32[]{:S(2)}) collective-permute-start(bf16[1024,256]{1,0:T(8,128)(2,1)S(1)} %collective-permute-done.22.refs_10_.refs_11_), channel_id=1, source_target_pairs={{0,1},{1,0},{2,3},{3,2},{4,5},{5,4},{6,7},{7,6},{8,9},{9,8},{10,11... | collective-permute-start | bytes 1572872 | tf_op jit(solution)/shard_map/ppermute | solution.py:26
  87.0 6.8 %collective-permute-start.18 = (bf16[512,256]{1,0:T(8,128)(2,1)S(1)}, bf16[512,256]{1,0:T(8,128)(2,1)S(1)}, u32[]{:S(2)}, u32[]{:S(2)}) collective-permute-start(bf16[512,256]{1,0:T(8,128)(2,1)S(1)} %get-tuple-element.61), channel_id=1, source_target_pairs={{0,1},{1,0},{2,3},{3,2},{4,5},{5,4},{6,7},{7,6},{8,9},{9,8},{10,11... | collective-permute-start | bytes 786440 | tf_op jit(solution)/shard_map/ppermute | solution.py:26
  93.8 1.5 collective-permute-start.20
  103.2 14.2 %collective-permute-start.32 = (bf16[256,1024]{1,0:T(8,128)(2,1)}, bf16[256,1024]{1,0:T(8,128)(2,1)S(1)}, u32[]{:S(2)}, u32[]{:S(2)}) collective-permute-start(bf16[256,1024]{1,0:T(8,128)(2,1)} %get-tuple-element.65), channel_id=1, source_target_pairs={{0,4},{4,0},{1,5},{5,1},{2,6},{6,2},{3,7},{7,3},{8,12},{12,8},{9,1... | collective-permute-start | bytes 1572872 | tf_op jit(solution)/shard_map/ppermute | solution.py:26
  117.4 1.9 collective-permute-start.33
  151.5 2.9 %collective-permute-start.35 = (bf16[512,1024]{1,0:T(8,128)(2,1)}, bf16[512,1024]{1,0:T(8,128)(2,1)S(1)}, u32[]{:S(2)}, u32[]{:S(2)}) collective-permute-start(bf16[512,1024]{1,0:T(8,128)(2,1)} %get-tuple-element.69), channel_id=1, source_target_pairs={{0,1},{1,0},{2,3},{3,2},{4,5},{5,4},{6,7},{7,6},{8,9},{9,8},{10,11... | collective-permute-start | bytes 3145736 | tf_op jit(solution)/shard_map/ppermute | solution.py:26
  151.7 5.1 %collective-permute-start.34 = (bf16[512,1024]{1,0:T(8,128)(2,1)}, bf16[512,1024]{1,0:T(8,128)(2,1)S(1)}, u32[]{:S(2)}, u32[]{:S(2)}) collective-permute-start(bf16[512,1024]{1,0:T(8,128)(2,1)} %get-tuple-element.67), channel_id=1, source_target_pairs={{0,1},{1,0},{2,3},{3,2},{4,5},{5,4},{6,7},{7,6},{8,9},{9,8},{10,11... | collective-permute-start | bytes 3145736 | tf_op jit(solution)/shard_map/ppermute | solution.py:26
  155.7 14.0 %collective-permute-start.37 = (bf16[256,1024]{1,0:T(8,128)(2,1)S(1)}, bf16[256,1024]{1,0:T(8,128)(2,1)S(1)}, u32[]{:S(2)}, u32[]{:S(2)}) collective-permute-start(bf16[256,1024]{1,0:T(8,128)(2,1)S(1)} %onward.5.refs_2_), channel_id=1, source_target_pairs={{0,4},{4,0},{1,5},{5,1},{2,6},{6,2},{3,7},{7,3},{8,12},{12,8},{9,1... | collective-permute-start | bytes 1572872 | tf_op jit(solution)/shard_map/ppermute | solution.py:26
  156.7 23.8 %collective-permute-start.43 = (bf16[256,1536]{1,0:T(8,128)(2,1)S(1)}, bf16[256,1536]{1,0:T(8,128)(2,1)S(1)}, u32[]{:S(2)}, u32[]{:S(2)}) collective-permute-start(bf16[256,1536]{1,0:T(8,128)(2,1)S(1)} %copy-done.86), channel_id=1, source_target_pairs={{0,8},{8,0},{16,24},{24,16},{1,9},{9,1},{17,25},{25,17},{2,10},{10... | collective-permute-start | bytes 2359304 | tf_op jit(solution)/shard_map/ppermute | solution.py:72
  169.9 7.6 %collective-permute-start.38 = (bf16[128,1024]{1,0:T(8,128)(2,1)S(1)}, bf16[128,1024]{1,0:T(8,128)(2,1)S(1)}, u32[]{:S(2)}, u32[]{:S(2)}) collective-permute-start(bf16[128,1024]{1,0:T(8,128)(2,1)S(1)} %onward.7), channel_id=1, source_target_pairs={{0,2},{2,0},{1,3},{3,1},{4,6},{6,4},{5,7},{7,5},{8,10},{10,8},{9,1... | collective-permute-start | bytes 786440 | tf_op jit(solution)/shard_map/ppermute | solution.py:26
  171.5 14.1 %collective-permute-start.36 = (bf16[256,1024]{1,0:T(8,128)(2,1)S(1)}, bf16[256,1024]{1,0:T(8,128)(2,1)S(1)}, u32[]{:S(2)}, u32[]{:S(2)}) collective-permute-start(bf16[256,1024]{1,0:T(8,128)(2,1)S(1)} %onward.6.refs_3_), channel_id=1, source_target_pairs={{0,4},{4,0},{1,5},{5,1},{2,6},{6,2},{3,7},{7,3},{8,12},{12,8},{9,1... | collective-permute-start | bytes 1572872 | tf_op jit(solution)/shard_map/ppermute | solution.py:26
  179.0 6.6 %collective-permute-start.41 = (bf16[128,1024]{1,0:T(8,128)(2,1)S(1)}, bf16[128,1024]{1,0:T(8,128)(2,1)S(1)}, u32[]{:S(2)}, u32[]{:S(2)}) collective-permute-start(bf16[128,1024]{1,0:T(8,128)(2,1)S(1)} %get-tuple-element.72.refs_3_.refs_2_.refs_1_), channel_id=1, source_target_pairs={{0,2},{2,0},{1,3},{3,1},{4,6},{6,4},{5,7},{7,5},{8,10},{10,8},{9,1... | collective-permute-start | bytes 786440 | tf_op jit(solution)/shard_map/ppermute | solution.py:26
  180.5 34.4 %collective-permute-start.55 = (bf16[256,1536]{1,0:T(8,128)(2,1)S(1)}, bf16[256,1536]{1,0:T(8,128)(2,1)S(1)}, u32[]{:S(2)}, u32[]{:S(2)}) collective-permute-start(bf16[256,1536]{1,0:T(8,128)(2,1)S(1)} %copy-done.85), channel_id=1, source_target_pairs={{0,8},{8,0},{16,24},{24,16},{1,9},{9,1},{17,25},{25,17},{2,10},{10... | collective-permute-start | bytes 2359304 | tf_op jit(solution)/shard_map/ppermute | solution.py:72
  180.9 34.0 %collective-permute-start.56 = (bf16[256,1536]{1,0:T(8,128)(2,1)S(1)}, bf16[256,1536]{1,0:T(8,128)(2,1)S(1)}, u32[]{:S(2)}, u32[]{:S(2)}) collective-permute-start(bf16[256,1536]{1,0:T(8,128)(2,1)S(1)} %merge.6.refs_24_), channel_id=1, source_target_pairs={{0,16},{8,24},{16,0},{24,8},{1,17},{9,25},{17,1},{25,9},{2,18},{10... | collective-permute-start | bytes 2359304 | tf_op jit(solution)/shard_map/ppermute | solution.py:72
  183.1 3.4 %collective-permute-start.40 = (bf16[128,1024]{1,0:T(8,128)(2,1)S(1)}, bf16[128,1024]{1,0:T(8,128)(2,1)S(1)}, u32[]{:S(2)}, u32[]{:S(2)}) collective-permute-start(bf16[128,1024]{1,0:T(8,128)(2,1)S(1)} %get-tuple-element.72.refs_3_.refs_2_.refs_1_), channel_id=1, source_target_pairs={{0,1},{1,0},{2,3},{3,2},{4,5},{5,4},{6,7},{7,6},{8,9},{9,8},{10,11... | collective-permute-start | bytes 786440 | tf_op jit(solution)/shard_map/ppermute | solution.py:26
  185.6 1.5 collective-permute-start.42
  200.4 9.2 %collective-permute-start.48 = (bf16[128,1024]{1,0:T(8,128)(2,1)S(1)}, bf16[128,1024]{1,0:T(8,128)(2,1)S(1)}, u32[]{:S(2)}, u32[]{:S(2)}) collective-permute-start(bf16[128,1024]{1,0:T(8,128)(2,1)S(1)} %get-tuple-element.92), channel_id=1, source_target_pairs={{0,4},{4,0},{1,5},{5,1},{2,6},{6,2},{3,7},{7,3},{8,12},{12,8},{9,1... | collective-permute-start | bytes 786440 | tf_op jit(solution)/shard_map/ppermute | solution.py:26
  201.0 23.6 %collective-permute-start.44 = (bf16[256,1024]{1,0:T(8,128)(2,1)}, bf16[256,1024]{1,0:T(8,128)(2,1)}, u32[]{:S(2)}, u32[]{:S(2)}) collective-permute-start(bf16[256,1024]{1,0:T(8,128)(2,1)} %get-tuple-element.81), channel_id=1, source_target_pairs={{0,1},{1,0},{2,3},{3,2},{4,5},{5,4},{6,7},{7,6},{8,9},{9,8},{10,11... | collective-permute-start | bytes 1572872 | tf_op jit(solution)/shard_map/ppermute | solution.py:26
  201.0 18.3 %collective-permute-start.47 = (bf16[128,1024]{1,0:T(8,128)(2,1)S(1)}, bf16[128,1024]{1,0:T(8,128)(2,1)S(1)}, u32[]{:S(2)}, u32[]{:S(2)}) collective-permute-start(bf16[128,1024]{1,0:T(8,128)(2,1)S(1)} %get-tuple-element.90), channel_id=1, source_target_pairs={{0,4},{4,0},{1,5},{5,1},{2,6},{6,2},{3,7},{7,3},{8,12},{12,8},{9,1... | collective-permute-start | bytes 786440 | tf_op jit(solution)/shard_map/ppermute | solution.py:26
  216.8 20.2 %collective-permute-start.57 = (bf16[128,1536]{1,0:T(8,128)(2,1)}, bf16[128,1536]{1,0:T(8,128)(2,1)}, u32[]{:S(2)}, u32[]{:S(2)}) collective-permute-start(bf16[128,1536]{1,0:T(8,128)(2,1)} %get-tuple-element.102), channel_id=1, source_target_pairs={{0,4},{4,0},{1,5},{5,1},{2,6},{6,2},{3,7},{7,3},{8,12},{12,8},{9,1... | collective-permute-start | bytes 1179656 | tf_op jit(solution)/shard_map/ppermute | solution.py:26
  217.3 8.9 %collective-permute-start.39 = (bf16[128,1024]{1,0:T(8,128)(2,1)}, bf16[128,1024]{1,0:T(8,128)(2,1)}, u32[]{:S(2)}, u32[]{:S(2)}) collective-permute-start(bf16[128,1024]{1,0:T(8,128)(2,1)} %onward.8.refs_23_), channel_id=1, source_target_pairs={{0,2},{2,0},{1,3},{3,1},{4,6},{6,4},{5,7},{7,5},{8,10},{10,8},{9,1... | collective-permute-start | bytes 786440 | tf_op jit(solution)/shard_map/ppermute | solution.py:26
  217.8 16.9 %collective-permute-start.50 = (bf16[128,1024]{1,0:T(8,128)(2,1)}, bf16[128,1024]{1,0:T(8,128)(2,1)}, u32[]{:S(2)}, u32[]{:S(2)}) collective-permute-start(bf16[128,1024]{1,0:T(8,128)(2,1)} %get-tuple-element.94), channel_id=1, source_target_pairs={{0,4},{4,0},{1,5},{5,1},{2,6},{6,2},{3,7},{7,3},{8,12},{12,8},{9,1... | collective-permute-start | bytes 786440 | tf_op jit(solution)/shard_map/ppermute | solution.py:26
  220.0 15.3 %collective-permute-start.51 = (bf16[128,1024]{1,0:T(8,128)(2,1)}, bf16[128,1024]{1,0:T(8,128)(2,1)}, u32[]{:S(2)}, u32[]{:S(2)}) collective-permute-start(bf16[128,1024]{1,0:T(8,128)(2,1)} %merge.7.refs_2_.refs_3_), channel_id=1, source_target_pairs={{0,8},{8,0},{16,24},{24,16},{1,9},{9,1},{17,25},{25,17},{2,10},{10... | collective-permute-start | bytes 786440 | tf_op jit(solution)/shard_map/ppermute | solution.py:72
  224.6 25.0 %collective-permute-start.46 = (bf16[128,1024]{1,0:T(8,128)(2,1)}, bf16[128,1024]{1,0:T(8,128)(2,1)}, u32[]{:S(2)}, u32[]{:S(2)}) collective-permute-start(bf16[128,1024]{1,0:T(8,128)(2,1)} %get-tuple-element.88), channel_id=1, source_target_pairs={{0,4},{4,0},{1,5},{5,1},{2,6},{6,2},{3,7},{7,3},{8,12},{12,8},{9,1... | collective-permute-start | bytes 786440 | tf_op jit(solution)/shard_map/ppermute | solution.py:26
  226.3 23.4 %collective-permute-start.49 = (bf16[128,1024]{1,0:T(8,128)(2,1)}, bf16[128,1024]{1,0:T(8,128)(2,1)}, u32[]{:S(2)}, u32[]{:S(2)}) collective-permute-start(bf16[128,1024]{1,0:T(8,128)(2,1)} %merge.8), channel_id=1, source_target_pairs={{0,8},{8,0},{16,24},{24,16},{1,9},{9,1},{17,25},{25,17},{2,10},{10... | collective-permute-start | bytes 786440 | tf_op jit(solution)/shard_map/ppermute | solution.py:72
  234.8 6.4 %collective-permute-start.45 = (bf16[128,1024]{1,0:T(8,128)(2,1)S(1)}, bf16[128,1024]{1,0:T(8,128)(2,1)S(1)}, u32[]{:S(2)}, u32[]{:S(2)}) collective-permute-start(bf16[128,1024]{1,0:T(8,128)(2,1)S(1)} %onward.9.refs_9_), channel_id=1, source_target_pairs={{0,2},{2,0},{1,3},{3,1},{4,6},{6,4},{5,7},{7,5},{8,10},{10,8},{9,1... | collective-permute-start | bytes 786440 | tf_op jit(solution)/shard_map/ppermute | solution.py:26
  236.4 13.3 %collective-permute-start.52 = (bf16[128,1024]{1,0:T(8,128)(2,1)S(1)}, bf16[128,1024]{1,0:T(8,128)(2,1)S(1)}, u32[]{:S(2)}, u32[]{:S(2)}) collective-permute-start(bf16[128,1024]{1,0:T(8,128)(2,1)S(1)} %merge.9), channel_id=1, source_target_pairs={{0,16},{8,24},{16,0},{24,8},{1,17},{9,25},{17,1},{25,9},{2,18},{10... | collective-permute-start | bytes 786440 | tf_op jit(solution)/shard_map/ppermute | solution.py:72
  238.9 32.9 %collective-permute-start.58 = (bf16[128,1024]{1,0:T(8,128)(2,1)}, bf16[128,1024]{1,0:T(8,128)(2,1)}, u32[]{:S(2)}, u32[]{:S(2)}) collective-permute-start(bf16[128,1024]{1,0:T(8,128)(2,1)} %get-tuple-element.135), channel_id=1, source_target_pairs={{1,2},{2,1},{5,6},{6,5},{9,10},{10,9},{13,14},{14,13},{17,18},{18,... | collective-permute-start | bytes 786440 | tf_op jit(solution)/shard_map/ppermute | solution.py:957
  241.1 30.6 %collective-permute-start.59 = (bf16[128,1024]{1,0:T(8,128)(2,1)}, bf16[128,1024]{1,0:T(8,128)(2,1)}, u32[]{:S(2)}, u32[]{:S(2)}) collective-permute-start(bf16[128,1024]{1,0:T(8,128)(2,1)} %get-tuple-element.134), channel_id=1, source_target_pairs={{0,2},{1,0},{2,3},{3,1},{4,6},{5,4},{6,7},{7,5},{8,10},{9,8},{10,1... | collective-permute-start | bytes 786440 | tf_op jit(solution)/shard_map/ppermute | solution.py:958
  244.6 12.2 %all-to-all-start.1 = ((f32[32,1,1024]{2,1,0:T(1,128)}), f32[32,1,1024]{2,1,0:T(1,128)S(1)}, u32[]{:S(2)}, u32[]{:S(2)}) async-start(f32[32,1,1024]{2,1,0:T(1,128)} %get-tuple-element.103), calls=%async_computation.1 | async-start | bytes 262144 | tf_op jit(solution)/shard_map/all_to_all | solution.py:907
  256.8 28.9 %all-to-all-start = ((f32[32,5,1024]{2,1,0:T(8,128)}), f32[32,5,1024]{2,1,0:T(8,128)S(1)}, u32[]{:S(2)}, u32[]{:S(2)}) async-start(f32[32,5,1024]{2,1,0:T(8,128)} %get-tuple-element.83), calls=%async_computation | async-start | bytes 2097152 | tf_op jit(solution)/shard_map/all_to_all | solution.py:907
  259.5 10.1 %collective-permute-start.53 = (bf16[128,256]{1,0:T(8,128)(2,1)S(1)}, bf16[128,256]{1,0:T(8,128)(2,1)S(1)}, u32[]{:S(2)}, u32[]{:S(2)}) collective-permute-start(bf16[128,256]{1,0:T(8,128)(2,1)S(1)} %broadcast_select_fusion.18), channel_id=1, source_target_pairs={{0,2},{2,0},{1,3},{3,1},{4,6},{6,4},{5,7},{7,5},{8,10},{10,8},{9,1... | collective-permute-start | bytes 196616 | tf_op jit(solution)/shard_map/ppermute | solution.py:26
  269.7 1.3 collective-permute-start.54
  (85 other events, 814.8 us)
where the time goes:
time: 287 us; the launch traced here: 288 us
  waiting for transfers between devices  125 us (44%)
  Pallas kernels  72.3 us (25%)
  starting transfers between devices  60.1 us (21%)
  local copies, waits for them, and re-layouts  14.7 us (5%)
  other arithmetic  12.8 us (4%)
    ppermute x45, waiting for transfers between devices, swap(): return lax.ppermute(x, axis, SWAP)  75.7 us
    pallas_call x21, Pallas kernels, call(): pl.pallas_call(kernel, out_shape=[jax.ShapeDtypeStruct(shape, dtype) for...  72.3 us
    ppermute x45, starting transfers between devices, swap(): return lax.ppermute(x, axis, SWAP)  33.6 us
    ppermute x12, waiting for transfers between devices, swap_far(): return lax.ppermute(x, FAR, [(i, i ^ bit) for i in range(far_count())])  32.7 us
    ppermute x12, starting transfers between devices, swap_far(): return lax.ppermute(x, FAR, [(i, i ^ bit) for i in range(far_count())])  16.7 us
    all_to_all x2, waiting for transfers between devices, everywhere(): return lax.all_to_all(vectors, ALL, 0, 0, tiled=True)  16.4 us
    unnamed x175, local copies, waits for them, and re-layouts  11.7 us
    all_to_all x2, starting transfers between devices, everywhere(): return lax.all_to_all(vectors, ALL, 0, 0, tiled=True)  6.64 us
  transfers between devices with their start and end apart: 62, of which 23 were waited for; matrix products, arithmetic and copies ran while one was open for 5% of the time, Pallas kernels for 13%

commit v1 on v0

--- a/solution.py
+++ b/solution.py
@@ -115,6 +115,7 @@
 BLOCK = 128
 PIECES = 8
 LINE = 4
+ROWS = 6
 MICROSECONDS = dict(
     attend=9, residual=3, mlp=11, middle=2, finish=2, attend_back=11, last=2, rows=1, onward=1, merge=1, weight_grad=2,
     fence=1, tick=0, totals=1, out=0,
@@ -402,20 +403,15 @@
     rows[3:4, :] = jnp.sum(total * branch_one[...], axis=0, keepdims=True)
 
 
-def finish_kernel(
-    speaker, keep, got, got_near, got_pair, own_grad, residual, rows_in, scale_two, output, spread
-):
+def finish_kernel(speaker, keep, got, got_near, got_pair, own_grad, residual, rows_in, scale_two, output, rows):
     branch_two = own_sum(keep, got, got_near, got_pair)
     result = residual[...] + scale_two[...] * branch_two
     output[...] = result.astype(bf16)
-    width = residual.shape[1]
-    power = jnp.sum(result * result, axis=0, keepdims=True)
-    scale_grad = jnp.sum(own_grad[...].astype(f32) * branch_two, axis=0, keepdims=True)
-    for i in range(spread.shape[0]):
-        spread[i, 0:1, :] = power
-        spread[i, 1:2, :] = scale_grad
-        spread[i, 2:4, :] = rows_in[2:4, :]
-        spread[i, 4:5, :] = jnp.full((1, width), speaker[0], jnp.int32).astype(f32)
+    rows[0:1, :] = jnp.sum(result * result, axis=0, keepdims=True)
+    rows[1:2, :] = jnp.sum(own_grad[...].astype(f32) * branch_two, axis=0, keepdims=True)
+    rows[2:4, :] = rows_in[2:4, :]
+    rows[4:5, :] = jnp.full((1, residual.shape[1]), speaker[0], jnp.int32).astype(f32)
+    rows[5:8, :] = jnp.zeros((3, residual.shape[1]), f32)
 
 
 def attend_back_kernel(bounds, own, core, across, both, qkv, stat, cos, sin, *refs):
@@ -503,7 +499,7 @@
         out[:, 3 * group :] = tdot(attended[:, cols], grads[:, lanes(shard, group)]).astype(bf16)
 
 
-def last_kernel(keep, got_core, got_pair, frames, residual_grad, gain_one, frames_grad, spread):
+def last_kernel(keep, got_core, got_pair, frames, residual_grad, gain_one, rows, frames_grad, spread, block):
     incoming = keep[:BLOCK, :] + got_core[:BLOCK, :].astype(f32) + got_pair[...].astype(f32)
     unit, inverse = normalise(frames[...].astype(f32))
     scaled = incoming * gain_one[...]
@@ -514,8 +510,13 @@
     )
     frames_grad[...] = (residual_grad[...] + back).astype(bf16)
     row = jnp.sum(incoming * unit, axis=0, keepdims=True)
+    for j in range(8):
+        at = slice(j * BLOCK, (j + 1) * BLOCK)
+        for r in range(ROWS - 1):
+            block[r * 8 + j : r * 8 + j + 1, :] = rows[r : r + 1, at]
+        block[(ROWS - 1) * 8 + j : (ROWS - 1) * 8 + j + 1, :] = row[:, at]
     for i in range(spread.shape[0]):
-        spread[i] = row
+        spread[i] = block[...].astype(spread.dtype)
 
 
 def copy_kernel(*refs):
@@ -570,9 +571,9 @@
         out[...] = total.astype(out.dtype)
 
 
-def totals_kernel(rows, power, gain, one, two):
+def totals_kernel(rows, power, sums):
     count = rows.shape[0]
-    ids = rows[:, 4, 0:1].astype(jnp.int32)
+    ids = rows[:, 4 * 8, 0:1].astype(f32).astype(jnp.int32)
     lane = lax.broadcasted_iota(jnp.int32, (count, SPEAKERS), 1)
     one_hot = (lane == ids).astype(f32)
 
@@ -581,12 +582,14 @@
             one_hot, x, (((0,), (0,)), ((), ())), precision=highest, preferred_element_type=f32
         )
 
-    sums = per_speaker(rows[:, 0, :])
     frames = per_speaker(jnp.full((count, BLOCK), float(BLOCK), f32))
-    power[...] = sums / jnp.maximum(frames[:, 0:1], 1.0)
-    two[...] = jnp.sum(rows[:, 1, :], axis=0, keepdims=True)
-    gain[...] = jnp.sum(rows[:, 2, :], axis=0, keepdims=True)
-    one[...] = jnp.sum(rows[:, 3, :], axis=0, keepdims=True)
+    share = 1.0 / jnp.maximum(frames, 1.0)
+    for j in range(8):
+        power[:, j * BLOCK : (j + 1) * BLOCK] = per_speaker(rows[:, j, :].astype(f32)) * share
+    total = rows[0].astype(f32)
+    for i in range(1, count):
+        total = total + rows[i].astype(f32)
+    sums[...] = total
 
 
 def kernel_pieces(pieces):
@@ -653,15 +656,15 @@
     return jnp.concatenate(out, axis=0)
 
 
-def sum_wide(own, other, outs):
+def sum_wide(own, other, outs, after=()):
     if far_count() != LINE:
         return sum_wide_long(own, other, outs), []
     whole = [(own[0].shape[1], bf16)]
     near = [swap(x, NEAR) for x in other]
-    third = merge([own[3], near[3]], whole)
+    third = merge([own[3], near[3]], whole, after)
     halfway = merge([own[2], near[2], swap_far(third[0], 1)], whole)[0]
     first = merge([own[1], near[1]], whole, third)[0]
-    return merge([own[0], near[0], swap_far(first, 1), swap_far(halfway, 2)], outs), third
+    return merge([own[0], near[0], swap_far(first, 1), swap_far(halfway, 2)], outs), [first]
 
 
 def sum_wide_long(own, other, outs):
@@ -813,8 +816,8 @@
         ],
         [*frames_all, att, att_core, att_pair, att_both, *outs, scale_one, gain_two],
         [pltpu.VMEM((tokens, width), f32)],
-        megabytes=52,
-        after=[line_b[1], line_b[3], *grad_all],
+        megabytes=36,
+        after=[line_b[3], *grad_all],
     )
 
     near_even = swap(normed_even, NEAR)
@@ -834,7 +837,7 @@
             pltpu.SemaphoreType.DMA((LINE,)),
         ],
         anywhere=range(11, 11 + LINE),
-        megabytes=52,
+        megabytes=36,
     )
 
     half_shape = ((2 * shard_len, width), bf16)
@@ -884,40 +887,37 @@
         ],
         smem=1,
         anywhere=range(9, 15 + PIECES),
-        megabytes=24,
         after=[to_pair_late, halfway_b],
     )
     own_a, other_a = grads_a[:4], grads_a[4:]
     got = swap(send, CORE)
     onward = call(onward_kernel, "onward", [((shard_len, width), bf16)], [keep, got])[0]
-    output, early_spread = call(
+    output, rows = call(
         finish_kernel,
         "finish",
-        [((shard_len, width), bf16), ((far_count() * 8, 5, width), f32)],
+        [((shard_len, width), bf16), ((8, width), f32)],
         [speaker.astype(jnp.int32), *met_late, grad_here, residual, rows, scale_two],
         smem=1,
-        after=[onward],
-    )
-    (query_sum, key_sum, value_sum, out_sum), third_a = sum_wide(
+    )
+    (query_sum, key_sum, value_sum, out_sum), passed_a = sum_wide(
         own_a, other_a, [(group, bf16)] * 3 + [(group, f32)]
     )
-    kept_b, left_b = split_rows(terms_b, third_a)
+    kept_b, left_b = split_rows(terms_b, passed_a)
     came_b = swap(left_b, NEAR)
-    def everywhere(vectors):
-        return lax.all_to_all(vectors, ALL, 0, 0, tiled=True)
-
-    early = everywhere(early_spread)
-    frames_grad, late_spread = call(
+    frames_grad, shared = call(
         last_kernel,
         "last",
-        [((shard_len, width), bf16), ((far_count() * 8, 1, width), f32)],
-        [keep, got, swap(onward, PAIR), frames_here, residual_grad, gain_one],
-        after=(),
-    )
-    late = everywhere(late_spread)
-    speaker_power, gain_two_grad, scale_one_grad, scale_two_grad = call(
-        totals_kernel, "totals", [((SPEAKERS, width), f32)] + [((1, width), f32)] * 3, [early]
-    )
+        [((shard_len, width), bf16), ((far_count() * 8, ROWS * 8, BLOCK), bf16)],
+        [keep, got, swap(onward, PAIR), frames_here, residual_grad, gain_one, rows],
+        [pltpu.VMEM((ROWS * 8, BLOCK), f32)],
+    )
+    speaker_power, sums = call(
+        totals_kernel,
+        "totals",
+        [((SPEAKERS, width), f32), ((ROWS * 8, BLOCK), f32)],
+        [lax.all_to_all(shared, ALL, 0, 0, tiled=True)],
+    )
+    sums = sums.reshape(ROWS, width)
 
     def near_order(kept, came):
         return jnp.concatenate(
@@ -941,10 +941,10 @@
         out_sum,
         gate_up_grad_out,
         down_grad,
-        jnp.sum(late[:, 0], axis=0),
-        gain_two_grad[0],
-        scale_one_grad[0],
-        scale_two_grad[0],
+        sums[5],
+        sums[2],
+        sums[3],
+        sums[1],
     )
 
 

time: 287 us -> 251 us (0.87); the launches traced: 288 us -> 246 us
  Pallas kernels: 72.3 us -> 50.1 us
  waiting for transfers between devices: 125 us -> 111 us
  other arithmetic: 12.8 us -> 9.76 us
    pallas_call x21, Pallas kernels: 72.3 us -> 50.1 us  [call(): pl.pallas_call(kernel, out_shape=[jax.ShapeDtypeStruct(shape, dtype) for...]
    all_to_all x2 -> x1, waiting for transfers between devices: 16.4 us -> 8.76 us  [body(): lax.all_to_all(shared, ALL, 0, 0, tiled=True)]
    ppermute x45, waiting for transfers between devices: 75.7 us -> 71.8 us  [swap(): return lax.ppermute(x, axis, SWAP)]
    all_to_all x2 -> x1, starting transfers between devices: 6.64 us -> 3.13 us  [body(): lax.all_to_all(shared, ALL, 0, 0, tiled=True)]
    unnamed x175 -> x123, local copies, waits for them, and re-layouts: 11.7 us -> 10.9 us
  transfers between devices with their start and end apart: 62 -> 61, of which waited for: 23 -> 24; matrix products, arithmetic and copies ran while one was open for 5% -> 5% of each run, Pallas kernels for 13% -> 13%
where the time goes in v1:
time: 251 us; the launch traced here: 246 us
  waiting for transfers between devices  111 us (44%)
  starting transfers between devices  57.9 us (23%)
  Pallas kernels  50.1 us (20%)
  local copies, waits for them, and re-layouts  14.4 us (6%)
  other arithmetic  9.76 us (4%)
  between operations  2.74 us (1%)
    ppermute x45, waiting for transfers between devices, swap(): return lax.ppermute(x, axis, SWAP)  71.8 us
    pallas_call x21, Pallas kernels, call(): pl.pallas_call(kernel, out_shape=[jax.ShapeDtypeStruct(shape, dtype) for...  50.1 us
    ppermute x45, starting transfers between devices, swap(): return lax.ppermute(x, axis, SWAP)  34.8 us
    ppermute x12, waiting for transfers between devices, swap_far(): return lax.ppermute(x, FAR, [(i, i ^ bit) for i in range(far_count())])  30.8 us
    ppermute x12, starting transfers between devices, swap_far(): return lax.ppermute(x, FAR, [(i, i ^ bit) for i in range(far_count())])  16.9 us
    unnamed x123, local copies, waits for them, and re-layouts  10.9 us
    all_to_all x1, waiting for transfers between devices, body(): lax.all_to_all(shared, ALL, 0, 0, tiled=True)  8.76 us
  transfers between devices with their start and end apart: 61, of which 24 were waited for; matrix products, arithmetic and copies ran while one was open for 5% of the time, Pallas kernels for 13%

profile of v1, /device:TPU:0, one launch (start us, length us, event | category | flops | bytes accessed | tf_op | source)
XLA Modules:
  0.0 246.3 jit_solution(13662306060998199424)
XLA Ops:
  0.7 1.1 reshape.291
  5.5 2.6 %collective-permute-start.1 = (bf16[64,1024]{1,0:T(8,128)(2,1)S(1)}, bf16[64,1024]{1,0:T(8,128)(2,1)S(1)}, u32[]{:S(2)}, u32[]{:S(2)}) collective-permute-start(bf16[64,1024]{1,0:T(8,128)(2,1)S(1)} %select_bitcast_fusion.4), channel_id=1, source_target_pairs={{0,2},{2,0},{1,3},{3,1},{4,6},{6,4},{5,7},{7,5},{8,10},{10,8},{9,1... | collective-permute-start | bytes 393224 | tf_op jit(solution)/shard_map/ppermute | solution.py:26
  8.5 1.6 collective-permute-start.13
  10.0 1.4 collective-permute-start.14
  12.4 2.9 %collective-permute-start.6 = (bf16[128,1024]{1,0:T(8,128)(2,1)S(1)}, bf16[128,1024]{1,0:T(8,128)(2,1)S(1)}, u32[]{:S(2)}, u32[]{:S(2)}) collective-permute-start(bf16[128,1024]{1,0:T(8,128)(2,1)S(1)} %pad_maximum_fusion.3.refs_2_.refs_0_.refs_5_.refs_13_), channel_id=1, source_target_pairs={{0,16},{8,24},{16,0},{24,8},{1,17},{9,25},{17,1},{25,9},{2,18},{10... | collective-permute-start | bytes 786440 | tf_op jit(solution)/shard_map/ppermute | solution.py:72
  15.2 1.6 collective-permute-start.5
  16.9 2.0 collective-permute-start.8
  18.8 1.7 collective-permute-done.14
  20.5 1.9 collective-permute-start.3
  22.7 4.5 %collective-permute-done.6.refs_2_.refs_7_.refs_15_ = bf16[128,1024]{1,0:T(8,128)(2,1)S(1)} collective-permute-done((bf16[128,1024]{1,0:T(8,128)(2,1)S(1)}, bf16[128,1024]{1,0:T(8,128)(2,1)S(1)}, u32[]{:S(2)}, u32[]{:S(2)}) %collective-permute-start.6) | collective-permute-done | bytes 262176 | tf_op jit(solution)/shard_map/ppermute | solution.py:72
  27.2 1.5 collective-permute-start.28
  30.0 1.5 collective-permute-start.16
  31.5 2.0 collective-permute-start.17
  34.7 1.5 collective-permute-start.9
  36.2 18.7 %collective-permute-done.7.refs_3_.refs_8_.refs_16_ = bf16[128,1024]{1,0:T(8,128)(2,1)} collective-permute-done((bf16[128,1024]{1,0:T(8,128)(2,1)S(1)}, bf16[128,1024]{1,0:T(8,128)(2,1)}, u32[]{:S(2)}, u32[]{:S(2)}) %collective-permute-start.7) | collective-permute-done | bytes 262176 | tf_op jit(solution)/shard_map/ppermute | solution.py:72
  56.1 1.5 collective-permute-start.26
  57.8 3.8 %collective-permute-done.11.refs_7_.refs_12_.refs_20_ = bf16[128,1024]{1,0:T(8,128)(2,1)} collective-permute-done((bf16[128,1024]{1,0:T(8,128)(2,1)}, bf16[128,1024]{1,0:T(8,128)(2,1)}, u32[]{:S(2)}, u32[]{:S(2)}) %collective-permute-start.11) | collective-permute-done | bytes 262176 | tf_op jit(solution)/shard_map/ppermute | solution.py:26
  63.5 1.2 out.1.refs_18_.refs_8_.refs_9_
  64.8 1.6 collective-permute-start.22
  67.0 2.2 collective-permute-done.16.refs_16_.refs_9_
  69.2 3.3 %collective-permute-start.24 = (bf16[256,1536]{1,0:T(8,128)(2,1)S(1)}, bf16[256,1536]{1,0:T(8,128)(2,1)S(1)}, u32[]{:S(2)}, u32[]{:S(2)}) collective-permute-start(bf16[256,1536]{1,0:T(8,128)(2,1)S(1)} %collective-permute-done.17.refs_17_.refs_10_), channel_id=1, source_target_pairs={{0,8},{8,0},{16,24},{24,16},{1,9},{9,1},{17,25},{25,17},{2,10},{10... | collective-permute-start | bytes 2359304 | tf_op jit(solution)/shard_map/ppermute | solution.py:72
  72.6 1.8 fusion
  74.5 10.2 %attend.1 = (bf16[512,1024]{1,0:T(8,128)(2,1)}, bf16[512,768]{1,0:T(8,128)(2,1)}, f32[512,128]{1,0:T(8,128)S(1)}, bf16[512,256]{1,0:T(8,128)(2,1)S(1)}, bf16[512...) custom-call(s32[1,2]{1,0:T(1,128)S(1)} %copy-done.55, bf16[128,1024]{1,0:T(8,128)(2,1)S(1)} %copy-done.24, ...), custom_call_target="tpu_custom_call" | custom-call | flops 900000000 | tf_op jit(solution)/shard_map/attend/pallas_call | solution.py:143
  85.9 1.5 collective-permute-start.19
  88.0 6.2 %collective-permute-done.19.refs_6_ = bf16[512,256]{1,0:T(8,128)(2,1)S(1)} collective-permute-done((bf16[512,256]{1,0:T(8,128)(2,1)S(1)}, bf16[512,256]{1,0:T(8,128)(2,1)S(1)}, u32[]{:S(2)}, u32[]{:S(2)}) %collective-permute-start.19) | collective-permute-done | bytes 262176 | tf_op jit(solution)/shard_map/ppermute | solution.py:26
  94.2 1.5 collective-permute-done.20.refs_7_
  95.8 1.0 copy-done.1
  97.8 3.3 %residual.1 = (bf16[512,1024]{1,0:T(8,128)(2,1)S(1)}, bf16[256,1024]{1,0:T(8,128)(2,1)S(1)}, bf16[512,1024]{1,0:T(8,128)(2,1)S(1)}, f32[128,1024]{1,0:T(8,128)S(1)}, f32[128,1024]{1,0:T(8,128)S(1)}) custom-call(bf16[128,1024]{1,0:T(8,128)(2,1)S(1)} %copy-done.24, bf16[128,1024]{1,0:T(8,128)(2,1)S(1)} %copy-done.37, ...), custom_call_target="tpu_custom_call" | custom-call | flops 300000000 | tf_op jit(solution)/shard_map/residual/pallas_call | solution.py:143
  101.7 13.4 %collective-permute-done.32.near_even = bf16[256,1024]{1,0:T(8,128)(2,1)S(1)} collective-permute-done((bf16[256,1024]{1,0:T(8,128)(2,1)S(1)}, bf16[256,1024]{1,0:T(8,128)(2,1)S(1)}, u32[]{:S(2)}, u32[]{:S(2)}) %collective-permute-start.32) | collective-permute-done | bytes 524320 | tf_op jit(solution)/shard_map/ppermute | solution.py:26
  115.2 1.9 collective-permute-done.33.near_odd
  117.1 12.2 %mlp.1 = (bf16[512,1024]{1,0:T(8,128)(2,1)S(1)}, bf16[512,1024]{1,0:T(8,128)(2,1)S(1)}, bf16[512,1024]{1,0:T(8,128)(2,1)S(1)}, bf16[512,1024]{1,0:T(8,128)(2,1)S...) custom-call(bf16[512,1024]{1,0:T(8,128)(2,1)S(1)} %get-tuple-element, ...), custom_call_target="tpu_custom_call" | custom-call | flops 1100000000 | tf_op jit(solution)/shard_map/mlp/pallas_call | solution.py:143
  129.9 2.1 collective-permute-done.35.got.refs_1_
  133.7 12.5 %collective-permute-done.37.refs_2_.got_near = bf16[256,1024]{1,0:T(8,128)(2,1)S(1)} collective-permute-done((bf16[256,1024]{1,0:T(8,128)(2,1)S(1)}, bf16[256,1024]{1,0:T(8,128)(2,1)S(1)}, u32[]{:S(2)}, u32[]{:S(2)}) %collective-permute-start.37) | collective-permute-done | bytes 524320 | tf_op jit(solution)/shard_map/ppermute | solution.py:26
  146.3 1.6 collective-permute-start.38
  148.4 5.5 %collective-permute-done.38.got_pair = bf16[128,1024]{1,0:T(8,128)(2,1)S(1)} collective-permute-done((bf16[128,1024]{1,0:T(8,128)(2,1)S(1)}, bf16[128,1024]{1,0:T(8,128)(2,1)S(1)}, u32[]{:S(2)}, u32[]{:S(2)}) %collective-permute-start.38) | collective-permute-done | bytes 262176 | tf_op jit(solution)/shard_map/ppermute | solution.py:26
  154.5 1.6 collective-permute-start.41
  156.4 3.4 %collective-permute-start.56 = (bf16[256,1536]{1,0:T(8,128)(2,1)S(1)}, bf16[256,1536]{1,0:T(8,128)(2,1)S(1)}, u32[]{:S(2)}, u32[]{:S(2)}) collective-permute-start(bf16[256,1536]{1,0:T(8,128)(2,1)S(1)} %merge.6.refs_24_), channel_id=1, source_target_pairs={{0,16},{8,24},{16,0},{24,8},{1,17},{9,25},{17,1},{25,9},{2,18},{10... | collective-permute-start | bytes 2359304 | tf_op jit(solution)/shard_map/ppermute | solution.py:72
  159.8 1.4 collective-permute-done.41.refs_3_
  162.8 13.3 %attend_back.1 = (f32[256,1024]{1,0:T(8,128)S(1)}, bf16[256,1024]{1,0:T(8,128)(2,1)}, bf16[128,1024]{1,0:T(8,128)(2,1)S(1)}, bf16[128,1024]{1,0:T(8,128)(2,1)S(1...) custom-call(s32[1,2]{1,0:T(1,128)S(1)} %copy-done.55, ...), custom_call_target="tpu_custom_call" | custom-call | flops 1100000000 | tf_op jit(solution)/shard_map/attend_back/pallas_call | solution.py:143
  176.7 1.5 collective-permute-start.47
  178.2 7.1 %collective-permute-done.48.refs_1_ = bf16[128,1024]{1,0:T(8,128)(2,1)S(1)} collective-permute-done((bf16[128,1024]{1,0:T(8,128)(2,1)S(1)}, bf16[128,1024]{1,0:T(8,128)(2,1)S(1)}, u32[]{:S(2)}, u32[]{:S(2)}) %collective-permute-start.48) | collective-permute-done | bytes 262176 | tf_op jit(solution)/shard_map/ppermute | solution.py:26
  186.1 4.1 %collective-permute-done.47.refs_1_ = bf16[128,1024]{1,0:T(8,128)(2,1)S(1)} collective-permute-done((bf16[128,1024]{1,0:T(8,128)(2,1)S(1)}, bf16[128,1024]{1,0:T(8,128)(2,1)S(1)}, u32[]{:S(2)}, u32[]{:S(2)}) %collective-permute-start.47) | collective-permute-done | bytes 262176 | tf_op jit(solution)/shard_map/ppermute | solution.py:26
  190.3 1.9 collective-permute-done.56.refs_2_
  195.1 1.5 collective-permute-start.50
  197.5 3.5 %collective-permute-done.39.got_pair = bf16[128,1024]{1,0:T(8,128)(2,1)} collective-permute-done((bf16[128,1024]{1,0:T(8,128)(2,1)S(1)}, bf16[128,1024]{1,0:T(8,128)(2,1)}, u32[]{:S(2)}, u32[]{:S(2)}) %collective-permute-start.39) | collective-permute-done | bytes 262176 | tf_op jit(solution)/shard_map/ppermute | solution.py:26
  201.1 1.0 copy-done.27
  202.1 1.0 copy-done.29
  203.1 2.0 finish.1
  205.1 1.5 collective-permute-start.46
  207.1 4.1 %collective-permute-done.50.refs_1_ = bf16[128,1024]{1,0:T(8,128)(2,1)} collective-permute-done((bf16[128,1024]{1,0:T(8,128)(2,1)}, bf16[128,1024]{1,0:T(8,128)(2,1)}, u32[]{:S(2)}, u32[]{:S(2)}) %collective-permute-start.50) | collective-permute-done | bytes 262176 | tf_op jit(solution)/shard_map/ppermute | solution.py:26
  211.2 1.3 collective-permute-start.45
  212.5 1.1 merge.9
  213.7 1.0 collective-permute-start.52
  214.7 1.0 broadcast_select_fusion.14
  216.7 1.4 collective-permute-start.58
  219.0 1.1 collective-permute-start.59
  220.1 3.5 %collective-permute-done.52.refs_3_ = bf16[128,1024]{1,0:T(8,128)(2,1)S(1)} collective-permute-done((bf16[128,1024]{1,0:T(8,128)(2,1)S(1)}, bf16[128,1024]{1,0:T(8,128)(2,1)S(1)}, u32[]{:S(2)}, u32[]{:S(2)}) %collective-permute-start.52) | collective-permute-done | bytes 262176 | tf_op jit(solution)/shard_map/ppermute | solution.py:72
  226.0 1.3 last.1
  227.4 3.1 %all-to-all-start = ((bf16[32,48,128]{2,1,0:T(8,128)(2,1)}), bf16[32,48,128]{2,1,0:T(8,128)(2,1)S(1)}, u32[]{:S(2)}, u32[]{:S(2)}) async-start(bf16[32,48,128]{2,1,0:T(8,128)(2,1)} %get-tuple-element.83), calls=%async_computation | async-start | bytes 786432 | tf_op jit(solution)/shard_map/all_to_all | solution.py:918
  230.9 1.0 collective-permute-done.54
  232.7 1.2 select_select_fusion.2
  233.9 1.1 maximum_convert_fusion
  234.9 8.8 %all-to-all-done.rows = bf16[32,48,128]{2,1,0:T(8,128)(2,1)S(1)} async-done(((bf16[32,48,128]{2,1,0:T(8,128)(2,1)}), bf16[32,48,128]{2,1,0:T(8,128)(2,1)S(1)}, u32[]{:S(2)}, u32[]{:S(2)}) %all-to-all-start) | async-done | bytes 393248 | tf_op jit(solution)/shard_map/all_to_all | solution.py:918
  243.7 1.6 totals.1
  (248 shorter events, 31.3 us)
Async XLA Ops:
  2.3 3.1 %collective-permute-start = (bf16[2,32,1024]{2,1,0:T(8,128)(2,1)S(1)}, bf16[2,32,1024]{2,1,0:T(8,128)(2,1)S(1)}, u32[]{:S(2)}, u32[]{:S(2)}) collective-permute-start(bf16[2,32,1024]{2,1,0:T(8,128)(2,1)S(1)} %pad_maximum_fusion.9), channel_id=1, source_target_pairs={{0,1},{1,0},{2,3},{3,2},{4,5},{5,4},{6,7},{7,6},{8,9},{9,8},{10,11... | collective-permute-start | bytes 393224 | tf_op jit(solution)/shard_map/ppermute | solution.py:26
  4.8 3.3 %collective-permute-start.12 = (bf16[2,32,3072]{2,1,0:T(8,128)(2,1)S(1)}, bf16[2,32,3072]{2,1,0:T(8,128)(2,1)S(1)}, u32[]{:S(2)}, u32[]{:S(2)}) collective-permute-start(bf16[2,32,3072]{2,1,0:T(8,128)(2,1)S(1)} %pad_maximum_fusion.2), channel_id=1, source_target_pairs={{0,1},{1,0},{2,3},{3,2},{4,5},{5,4},{6,7},{7,6},{8,9},{9,8},{10,11... | collective-permute-start | bytes 1179656 | tf_op jit(solution)/shard_map/ppermute | solution.py:26
  5.5 6.8 %collective-permute-start.1 = (bf16[64,1024]{1,0:T(8,128)(2,1)S(1)}, bf16[64,1024]{1,0:T(8,128)(2,1)S(1)}, u32[]{:S(2)}, u32[]{:S(2)}) collective-permute-start(bf16[64,1024]{1,0:T(8,128)(2,1)S(1)} %select_bitcast_fusion.4), channel_id=1, source_target_pairs={{0,2},{2,0},{1,3},{3,1},{4,6},{6,4},{5,7},{7,5},{8,10},{10,8},{9,1... | collective-permute-start | bytes 393224 | tf_op jit(solution)/shard_map/ppermute | solution.py:26
  8.5 8.4 %collective-permute-start.13 = (bf16[64,1536]{1,0:T(8,128)(2,1)S(1)}, bf16[64,1536]{1,0:T(8,128)(2,1)S(1)}, u32[]{:S(2)}, u32[]{:S(2)}) collective-permute-start(bf16[64,1536]{1,0:T(8,128)(2,1)S(1)} %get-tuple-element.121), channel_id=1, source_target_pairs={{0,4},{4,0},{1,5},{5,1},{2,6},{6,2},{3,7},{7,3},{8,12},{12,8},{9,1... | collective-permute-start | bytes 589832 | tf_op jit(solution)/shard_map/ppermute | solution.py:26
  10.0 10.5 %collective-permute-start.14 = (bf16[64,1536]{1,0:T(8,128)(2,1)S(1)}, bf16[64,1536]{1,0:T(8,128)(2,1)S(1)}, u32[]{:S(2)}, u32[]{:S(2)}) collective-permute-start(bf16[64,1536]{1,0:T(8,128)(2,1)S(1)} %get-tuple-element.122), channel_id=1, source_target_pairs={{0,2},{2,0},{1,3},{3,1},{4,6},{6,4},{5,7},{7,5},{8,10},{10,8},{9,1... | collective-permute-start | bytes 589832 | tf_op jit(solution)/shard_map/ppermute | solution.py:26
  11.5 11.0 %collective-permute-start.15 = (bf16[64,1536]{1,0:T(8,128)(2,1)S(1)}, bf16[64,1536]{1,0:T(8,128)(2,1)S(1)}, u32[]{:S(2)}, u32[]{:S(2)}) collective-permute-start(bf16[64,1536]{1,0:T(8,128)(2,1)S(1)} %get-tuple-element.120), channel_id=1, source_target_pairs={{0,6},{2,4},{4,2},{6,0},{1,7},{3,5},{5,3},{7,1},{8,14},{10,12},{12... | collective-permute-start | bytes 589832 | tf_op jit(solution)/shard_map/ppermute | solution.py:646
  12.4 49.2 %copy-start.3 = (bf16[128,1024]{1,0:T(8,128)(2,1)}, bf16[128,1024]{1,0:T(8,128)(2,1)S(1)}, u32[]{:S(2)}) copy-start(bf16[128,1024]{1,0:T(8,128)(2,1)S(1)} %pad_maximum_fusion.3.refs_2_.refs_0_.refs_5_.refs_13_) | copy-start | bytes 786436
  12.4 14.8 %collective-permute-start.6 = (bf16[128,1024]{1,0:T(8,128)(2,1)S(1)}, bf16[128,1024]{1,0:T(8,128)(2,1)S(1)}, u32[]{:S(2)}, u32[]{:S(2)}) collective-permute-start(bf16[128,1024]{1,0:T(8,128)(2,1)S(1)} %pad_maximum_fusion.3.refs_2_.refs_0_.refs_5_.refs_13_), channel_id=1, source_target_pairs={{0,16},{8,24},{16,0},{24,8},{1,17},{9,25},{17,1},{25,9},{2,18},{10... | collective-permute-start | bytes 786440 | tf_op jit(solution)/shard_map/ppermute | solution.py:72
  15.2 13.4 %collective-permute-start.5 = (bf16[128,1024]{1,0:T(8,128)(2,1)S(1)}, bf16[128,1024]{1,0:T(8,128)(2,1)S(1)}, u32[]{:S(2)}, u32[]{:S(2)}) collective-permute-start(bf16[128,1024]{1,0:T(8,128)(2,1)S(1)} %pad_maximum_fusion.3.refs_2_.refs_0_.refs_5_.refs_13_), channel_id=1, source_target_pairs={{0,8},{8,0},{16,24},{24,16},{1,9},{9,1},{17,25},{25,17},{2,10},{10... | collective-permute-start | bytes 786440 | tf_op jit(solution)/shard_map/ppermute | solution.py:72
  16.9 12.4 %collective-permute-start.8 = (bf16[128,1024]{1,0:T(8,128)(2,1)S(1)}, bf16[128,1024]{1,0:T(8,128)(2,1)S(1)}, u32[]{:S(2)}, u32[]{:S(2)}) collective-permute-start(bf16[128,1024]{1,0:T(8,128)(2,1)S(1)} %pad_maximum_fusion.3.refs_2_.refs_0_.refs_5_.refs_13_), channel_id=1, source_target_pairs={{0,4},{4,0},{1,5},{5,1},{2,6},{6,2},{3,7},{7,3},{8,12},{12,8},{9,1... | collective-permute-start | bytes 786440 | tf_op jit(solution)/shard_map/ppermute | solution.py:26
  20.5 10.9 %collective-permute-start.3 = (bf16[128,1024]{1,0:T(8,128)(2,1)S(1)}, bf16[128,1024]{1,0:T(8,128)(2,1)}, u32[]{:S(2)}, u32[]{:S(2)}) collective-permute-start(bf16[128,1024]{1,0:T(8,128)(2,1)S(1)} %get-tuple-element.57.refs_1_.refs_0_.frames), channel_id=1, source_target_pairs={{0,2},{2,0},{1,3},{3,1},{4,6},{6,4},{5,7},{7,5},{8,10},{10,8},{9,1... | collective-permute-start | bytes 786440 | tf_op jit(solution)/shard_map/ppermute | solution.py:26
  22.4 11.0 %collective-permute-start.2 = (bf16[128,1024]{1,0:T(8,128)(2,1)S(1)}, bf16[128,1024]{1,0:T(8,128)(2,1)S(1)}, u32[]{:S(2)}, u32[]{:S(2)}) collective-permute-start(bf16[128,1024]{1,0:T(8,128)(2,1)S(1)} %get-tuple-element.57.refs_1_.refs_0_.frames), channel_id=1, source_target_pairs={{0,1},{1,0},{2,3},{3,2},{4,5},{5,4},{6,7},{7,6},{8,9},{9,8},{10,11... | collective-permute-start | bytes 786440 | tf_op jit(solution)/shard_map/ppermute | solution.py:26
  27.2 37.6 %copy-start.11 = (bf16[128,1024]{1,0:T(8,128)(2,1)}, bf16[128,1024]{1,0:T(8,128)(2,1)S(1)}, u32[]{:S(2)}) copy-start(bf16[128,1024]{1,0:T(8,128)(2,1)S(1)} %collective-permute-done.6.refs_2_.refs_7_.refs_15_) | copy-start | bytes 786436
  27.2 7.5 %collective-permute-start.28 = (bf16[128,1024]{1,0:T(8,128)(2,1)S(1)}, bf16[128,1024]{1,0:T(8,128)(2,1)S(1)}, u32[]{:S(2)}, u32[]{:S(2)}) collective-permute-start(bf16[128,1024]{1,0:T(8,128)(2,1)S(1)} %get-tuple-element.61.refs_15_.refs_0_.own_grad), channel_id=1, source_target_pairs={{0,4},{4,0},{1,5},{5,1},{2,6},{6,2},{3,7},{7,3},{8,12},{12,8},{9,1... | collective-permute-start | bytes 786440 | tf_op jit(solution)/shard_map/ppermute | solution.py:26
  28.7 26.2 %collective-permute-start.7 = (bf16[128,1024]{1,0:T(8,128)(2,1)S(1)}, bf16[128,1024]{1,0:T(8,128)(2,1)}, u32[]{:S(2)}, u32[]{:S(2)}) collective-permute-start(bf16[128,1024]{1,0:T(8,128)(2,1)S(1)} %collective-permute-done.6.refs_2_.refs_7_.refs_15_), channel_id=1, source_target_pairs={{0,8},{8,0},{16,24},{24,16},{1,9},{9,1},{17,25},{25,17},{2,10},{10... | collective-permute-start | bytes 786440 | tf_op jit(solution)/shard_map/ppermute | solution.py:72
  30.0 39.2 %collective-permute-start.16 = (bf16[256,1536]{1,0:T(8,128)(2,1)S(1)}, bf16[256,1536]{1,0:T(8,128)(2,1)S(1)}, u32[]{:S(2)}, u32[]{:S(2)}) collective-permute-start(bf16[256,1536]{1,0:T(8,128)(2,1)S(1)} %pad_maximum_fusion.refs_8_), channel_id=1, source_target_pairs={{0,8},{8,0},{16,24},{24,16},{1,9},{9,1},{17,25},{25,17},{2,10},{10... | collective-permute-start | bytes 2359304 | tf_op jit(solution)/shard_map/ppermute | solution.py:72
  31.5 37.7 %collective-permute-start.17 = (bf16[256,1536]{1,0:T(8,128)(2,1)S(1)}, bf16[256,1536]{1,0:T(8,128)(2,1)S(1)}, u32[]{:S(2)}, u32[]{:S(2)}) collective-permute-start(bf16[256,1536]{1,0:T(8,128)(2,1)S(1)} %pad_maximum_fusion.refs_8_), channel_id=1, source_target_pairs={{0,16},{8,24},{16,0},{24,8},{1,17},{9,25},{17,1},{25,9},{2,18},{10... | collective-permute-start | bytes 2359304 | tf_op jit(solution)/shard_map/ppermute | solution.py:72
  34.1 21.3 %collective-permute-start.10 = (bf16[128,1024]{1,0:T(8,128)(2,1)S(1)}, bf16[128,1024]{1,0:T(8,128)(2,1)S(1)}, u32[]{:S(2)}, u32[]{:S(2)}) collective-permute-start(bf16[128,1024]{1,0:T(8,128)(2,1)S(1)} %collective-permute-done.6.refs_2_.refs_7_.refs_15_), channel_id=1, source_target_pairs={{0,4},{4,0},{1,5},{5,1},{2,6},{6,2},{3,7},{7,3},{8,12},{12,8},{9,1... | collective-permute-start | bytes 786440 | tf_op jit(solution)/shard_map/ppermute | solution.py:26
  34.7 23.0 %collective-permute-start.9 = (bf16[128,1024]{1,0:T(8,128)(2,1)S(1)}, bf16[128,1024]{1,0:T(8,128)(2,1)}, u32[]{:S(2)}, u32[]{:S(2)}) collective-permute-start(bf16[128,1024]{1,0:T(8,128)(2,1)S(1)} %collective-permute-done.5.refs_1_.refs_6_.refs_14_), channel_id=1, source_target_pairs={{0,4},{4,0},{1,5},{5,1},{2,6},{6,2},{3,7},{7,3},{8,12},{12,8},{9,1... | collective-permute-start | bytes 786440 | tf_op jit(solution)/shard_map/ppermute | solution.py:26
  54.9 6.7 %collective-permute-start.11 = (bf16[128,1024]{1,0:T(8,128)(2,1)}, bf16[128,1024]{1,0:T(8,128)(2,1)}, u32[]{:S(2)}, u32[]{:S(2)}) collective-permute-start(bf16[128,1024]{1,0:T(8,128)(2,1)} %collective-permute-done.7.refs_3_.refs_8_.refs_16_), channel_id=1, source_target_pairs={{0,4},{4,0},{1,5},{5,1},{2,6},{6,2},{3,7},{7,3},{8,12},{12,8},{9,1... | collective-permute-start | bytes 786440 | tf_op jit(solution)/shard_map/ppermute | solution.py:26
  56.1 8.6 %collective-permute-start.26 = (bf16[128,1024]{1,0:T(8,128)(2,1)S(1)}, bf16[128,1024]{1,0:T(8,128)(2,1)}, u32[]{:S(2)}, u32[]{:S(2)}) collective-permute-start(bf16[128,1024]{1,0:T(8,128)(2,1)S(1)} %get-tuple-element.61.refs_15_.refs_0_.own_grad), channel_id=1, source_target_pairs={{0,2},{2,0},{1,3},{3,1},{4,6},{6,4},{5,7},{7,5},{8,10},{10,8},{9,1... | collective-permute-start | bytes 786440 | tf_op jit(solution)/shard_map/ppermute | solution.py:26
  57.7 8.8 %collective-permute-start.25 = (bf16[128,1024]{1,0:T(8,128)(2,1)S(1)}, bf16[128,1024]{1,0:T(8,128)(2,1)S(1)}, u32[]{:S(2)}, u32[]{:S(2)}) collective-permute-start(bf16[128,1024]{1,0:T(8,128)(2,1)S(1)} %get-tuple-element.61.refs_15_.refs_0_.own_grad), channel_id=1, source_target_pairs={{0,1},{1,0},{2,3},{3,2},{4,5},{5,4},{6,7},{7,6},{8,9},{9,8},{10,11... | collective-permute-start | bytes 786440 | tf_op jit(solution)/shard_map/ppermute | solution.py:26
  61.6 5.4 %collective-permute-start.4 = (bf16[128,1024]{1,0:T(8,128)(2,1)}, bf16[128,1024]{1,0:T(8,128)(2,1)S(1)}, u32[]{:S(2)}, u32[]{:S(2)}) collective-permute-start(bf16[128,1024]{1,0:T(8,128)(2,1)} %collective-permute-done.3.refs_3_.refs_2_), channel_id=1, source_target_pairs={{0,1},{1,0},{2,3},{3,2},{4,5},{5,4},{6,7},{7,6},{8,9},{9,8},{10,11... | collective-permute-start | bytes 786440 | tf_op jit(solution)/shard_map/ppermute | solution.py:26
  64.8 22.7 %collective-permute-start.22 = (bf16[1024,256]{1,0:T(8,128)(2,1)S(1)}, bf16[1024,256]{1,0:T(8,128)(2,1)S(1)}, u32[]{:S(2)}, u32[]{:S(2)}) collective-permute-start(bf16[1024,256]{1,0:T(8,128)(2,1)S(1)} %out.1.refs_18_.refs_8_.refs_9_), channel_id=1, source_target_pairs={{0,2},{2,0},{1,3},{3,1},{4,6},{6,4},{5,7},{7,5},{8,10},{10,8},{9,1... | collective-permute-start | bytes 1572872 | tf_op jit(solution)/shard_map/ppermute | solution.py:26
  66.5 18.9 %collective-permute-start.30 = (bf16[128,1024]{1,0:T(8,128)(2,1)S(1)}, bf16[128,1024]{1,0:T(8,128)(2,1)S(1)}, u32[]{:S(2)}, u32[]{:S(2)}) collective-permute-start(bf16[128,1024]{1,0:T(8,128)(2,1)S(1)} %copy-done.34), channel_id=1, source_target_pairs={{0,2},{2,0},{1,3},{3,1},{4,6},{6,4},{5,7},{7,5},{8,10},{10,8},{9,1... | collective-permute-start | bytes 786440 | tf_op jit(solution)/shard_map/ppermute | solution.py:26
  67.0 18.9 %collective-permute-start.29 = (bf16[128,1024]{1,0:T(8,128)(2,1)S(1)}, bf16[128,1024]{1,0:T(8,128)(2,1)S(1)}, u32[]{:S(2)}, u32[]{:S(2)}) collective-permute-start(bf16[128,1024]{1,0:T(8,128)(2,1)S(1)} %copy-done.34), channel_id=1, source_target_pairs={{0,1},{1,0},{2,3},{3,2},{4,5},{5,4},{6,7},{7,6},{8,9},{9,8},{10,11... | collective-permute-start | bytes 786440 | tf_op jit(solution)/shard_map/ppermute | solution.py:26
  69.2 16.2 %collective-permute-start.27 = (bf16[128,1024]{1,0:T(8,128)(2,1)}, bf16[128,1024]{1,0:T(8,128)(2,1)S(1)}, u32[]{:S(2)}, u32[]{:S(2)}) collective-permute-start(bf16[128,1024]{1,0:T(8,128)(2,1)} %collective-permute-done.26.refs_17_.refs_2_), channel_id=1, source_target_pairs={{0,1},{1,0},{2,3},{3,2},{4,5},{5,4},{6,7},{7,6},{8,9},{9,8},{10,11... | collective-permute-start | bytes 786440 | tf_op jit(solution)/shard_map/ppermute | solution.py:26
  69.2 26.5 %collective-permute-start.24 = (bf16[256,1536]{1,0:T(8,128)(2,1)S(1)}, bf16[256,1536]{1,0:T(8,128)(2,1)S(1)}, u32[]{:S(2)}, u32[]{:S(2)}) collective-permute-start(bf16[256,1536]{1,0:T(8,128)(2,1)S(1)} %collective-permute-done.17.refs_17_.refs_10_), channel_id=1, source_target_pairs={{0,8},{8,0},{16,24},{24,16},{1,9},{9,1},{17,25},{25,17},{2,10},{10... | collective-permute-start | bytes 2359304 | tf_op jit(solution)/shard_map/ppermute | solution.py:72
  85.4 2.0 collective-permute-start.31
  85.4 8.8 %collective-permute-start.21 = (bf16[1024,256]{1,0:T(8,128)(2,1)}, bf16[1024,256]{1,0:T(8,128)(2,1)S(1)}, u32[]{:S(2)}, u32[]{:S(2)}) collective-permute-start(bf16[1024,256]{1,0:T(8,128)(2,1)} %copy-done), channel_id=1, source_target_pairs={{0,1},{1,0},{2,3},{3,2},{4,5},{5,4},{6,7},{7,6},{8,9},{9,8},{10,11... | collective-permute-start | bytes 1572872 | tf_op jit(solution)/shard_map/ppermute | solution.py:26
  85.9 8.3 %collective-permute-start.19 = (bf16[512,256]{1,0:T(8,128)(2,1)S(1)}, bf16[512,256]{1,0:T(8,128)(2,1)S(1)}, u32[]{:S(2)}, u32[]{:S(2)}) collective-permute-start(bf16[512,256]{1,0:T(8,128)(2,1)S(1)} %get-tuple-element.60), channel_id=1, source_target_pairs={{0,2},{2,0},{1,3},{3,1},{4,6},{6,4},{5,7},{7,5},{8,10},{10,8},{9,1... | collective-permute-start | bytes 786440 | tf_op jit(solution)/shard_map/ppermute | solution.py:26
  87.4 8.3 %collective-permute-start.23 = (bf16[1024,256]{1,0:T(8,128)(2,1)S(1)}, bf16[1024,256]{1,0:T(8,128)(2,1)S(1)}, u32[]{:S(2)}, u32[]{:S(2)}) collective-permute-start(bf16[1024,256]{1,0:T(8,128)(2,1)S(1)} %collective-permute-done.22.refs_10_.refs_11_), channel_id=1, source_target_pairs={{0,1},{1,0},{2,3},{3,2},{4,5},{5,4},{6,7},{7,6},{8,9},{9,8},{10,11... | collective-permute-start | bytes 1572872 | tf_op jit(solution)/shard_map/ppermute | solution.py:26
  87.5 6.8 %collective-permute-start.18 = (bf16[512,256]{1,0:T(8,128)(2,1)S(1)}, bf16[512,256]{1,0:T(8,128)(2,1)S(1)}, u32[]{:S(2)}, u32[]{:S(2)}) collective-permute-start(bf16[512,256]{1,0:T(8,128)(2,1)S(1)} %get-tuple-element.59), channel_id=1, source_target_pairs={{0,1},{1,0},{2,3},{3,2},{4,5},{5,4},{6,7},{7,6},{8,9},{9,8},{10,11... | collective-permute-start | bytes 786440 | tf_op jit(solution)/shard_map/ppermute | solution.py:26
  94.2 1.5 collective-permute-start.20
  101.1 52.8 %copy-start.28 = (f32[128,1024]{1,0:T(8,128)}, f32[128,1024]{1,0:T(8,128)S(1)}, u32[]{:S(2)}) copy-start(f32[128,1024]{1,0:T(8,128)S(1)} %get-tuple-element.68.residual) | copy-start | bytes 1572868
  101.1 14.0 %collective-permute-start.32 = (bf16[256,1024]{1,0:T(8,128)(2,1)S(1)}, bf16[256,1024]{1,0:T(8,128)(2,1)S(1)}, u32[]{:S(2)}, u32[]{:S(2)}) collective-permute-start(bf16[256,1024]{1,0:T(8,128)(2,1)S(1)} %get-tuple-element.63), channel_id=1, source_target_pairs={{0,4},{4,0},{1,5},{5,1},{2,6},{6,2},{3,7},{7,3},{8,12},{12,8},{9,1... | collective-permute-start | bytes 1572872 | tf_op jit(solution)/shard_map/ppermute | solution.py:26
  115.1 1.9 collective-permute-start.33
  129.3 2.7 %collective-permute-start.35 = (bf16[512,1024]{1,0:T(8,128)(2,1)S(1)}, bf16[512,1024]{1,0:T(8,128)(2,1)S(1)}, u32[]{:S(2)}, u32[]{:S(2)}) collective-permute-start(bf16[512,1024]{1,0:T(8,128)(2,1)S(1)} %get-tuple-element.67), channel_id=1, source_target_pairs={{0,1},{1,0},{2,3},{3,2},{4,5},{5,4},{6,7},{7,6},{8,9},{9,8},{10,11... | collective-permute-start | bytes 3145736 | tf_op jit(solution)/shard_map/ppermute | solution.py:26
  129.5 4.0 %collective-permute-start.34 = (bf16[512,1024]{1,0:T(8,128)(2,1)S(1)}, bf16[512,1024]{1,0:T(8,128)(2,1)S(1)}, u32[]{:S(2)}, u32[]{:S(2)}) collective-permute-start(bf16[512,1024]{1,0:T(8,128)(2,1)S(1)} %get-tuple-element.65), channel_id=1, source_target_pairs={{0,1},{1,0},{2,3},{3,2},{4,5},{5,4},{6,7},{7,6},{8,9},{9,8},{10,11... | collective-permute-start | bytes 3145736 | tf_op jit(solution)/shard_map/ppermute | solution.py:26
  132.2 14.0 %collective-permute-start.37 = (bf16[256,1024]{1,0:T(8,128)(2,1)S(1)}, bf16[256,1024]{1,0:T(8,128)(2,1)S(1)}, u32[]{:S(2)}, u32[]{:S(2)}) collective-permute-start(bf16[256,1024]{1,0:T(8,128)(2,1)S(1)} %onward.5.refs_2_), channel_id=1, source_target_pairs={{0,4},{4,0},{1,5},{5,1},{2,6},{6,2},{3,7},{7,3},{8,12},{12,8},{9,1... | collective-permute-start | bytes 1572872 | tf_op jit(solution)/shard_map/ppermute | solution.py:26
  132.8 23.3 %collective-permute-start.43 = (bf16[256,1536]{1,0:T(8,128)(2,1)S(1)}, bf16[256,1536]{1,0:T(8,128)(2,1)S(1)}, u32[]{:S(2)}, u32[]{:S(2)}) collective-permute-start(bf16[256,1536]{1,0:T(8,128)(2,1)S(1)} %get-tuple-element.78), channel_id=1, source_target_pairs={{0,8},{8,0},{16,24},{24,16},{1,9},{9,1},{17,25},{25,17},{2,10},{10... | collective-permute-start | bytes 2359304 | tf_op jit(solution)/shard_map/ppermute | solution.py:72
  146.3 7.6 %collective-permute-start.38 = (bf16[128,1024]{1,0:T(8,128)(2,1)S(1)}, bf16[128,1024]{1,0:T(8,128)(2,1)S(1)}, u32[]{:S(2)}, u32[]{:S(2)}) collective-permute-start(bf16[128,1024]{1,0:T(8,128)(2,1)S(1)} %onward.7), channel_id=1, source_target_pairs={{0,2},{2,0},{1,3},{3,1},{4,6},{6,4},{5,7},{7,5},{8,10},{10,8},{9,1... | collective-permute-start | bytes 786440 | tf_op jit(solution)/shard_map/ppermute | solution.py:26
  147.9 13.3 %collective-permute-start.36 = (bf16[256,1024]{1,0:T(8,128)(2,1)S(1)}, bf16[256,1024]{1,0:T(8,128)(2,1)S(1)}, u32[]{:S(2)}, u32[]{:S(2)}) collective-permute-start(bf16[256,1024]{1,0:T(8,128)(2,1)S(1)} %onward.6.refs_3_), channel_id=1, source_target_pairs={{0,4},{4,0},{1,5},{5,1},{2,6},{6,2},{3,7},{7,3},{8,12},{12,8},{9,1... | collective-permute-start | bytes 1572872 | tf_op jit(solution)/shard_map/ppermute | solution.py:26
  154.5 6.7 %collective-permute-start.41 = (bf16[128,1024]{1,0:T(8,128)(2,1)S(1)}, bf16[128,1024]{1,0:T(8,128)(2,1)S(1)}, u32[]{:S(2)}, u32[]{:S(2)}) collective-permute-start(bf16[128,1024]{1,0:T(8,128)(2,1)S(1)} %get-tuple-element.70.refs_3_.refs_2_.refs_1_), channel_id=1, source_target_pairs={{0,2},{2,0},{1,3},{3,1},{4,6},{6,4},{5,7},{7,5},{8,10},{10,8},{9,1... | collective-permute-start | bytes 786440 | tf_op jit(solution)/shard_map/ppermute | solution.py:26
  156.1 34.2 %collective-permute-start.55 = (bf16[256,1536]{1,0:T(8,128)(2,1)S(1)}, bf16[256,1536]{1,0:T(8,128)(2,1)S(1)}, u32[]{:S(2)}, u32[]{:S(2)}) collective-permute-start(bf16[256,1536]{1,0:T(8,128)(2,1)S(1)} %get-tuple-element.99), channel_id=1, source_target_pairs={{0,8},{8,0},{16,24},{24,16},{1,9},{9,1},{17,25},{25,17},{2,10},{10... | collective-permute-start | bytes 2359304 | tf_op jit(solution)/shard_map/ppermute | solution.py:72
  156.4 35.8 %collective-permute-start.56 = (bf16[256,1536]{1,0:T(8,128)(2,1)S(1)}, bf16[256,1536]{1,0:T(8,128)(2,1)S(1)}, u32[]{:S(2)}, u32[]{:S(2)}) collective-permute-start(bf16[256,1536]{1,0:T(8,128)(2,1)S(1)} %merge.6.refs_24_), channel_id=1, source_target_pairs={{0,16},{8,24},{16,0},{24,8},{1,17},{9,25},{17,1},{25,9},{2,18},{10... | collective-permute-start | bytes 2359304 | tf_op jit(solution)/shard_map/ppermute | solution.py:72
  159.8 2.2 collective-permute-start.40
  161.2 1.5 collective-permute-start.42
  176.1 9.2 %collective-permute-start.48 = (bf16[128,1024]{1,0:T(8,128)(2,1)S(1)}, bf16[128,1024]{1,0:T(8,128)(2,1)S(1)}, u32[]{:S(2)}, u32[]{:S(2)}) collective-permute-start(bf16[128,1024]{1,0:T(8,128)(2,1)S(1)} %get-tuple-element.91), channel_id=1, source_target_pairs={{0,4},{4,0},{1,5},{5,1},{2,6},{6,2},{3,7},{7,3},{8,12},{12,8},{9,1... | collective-permute-start | bytes 786440 | tf_op jit(solution)/shard_map/ppermute | solution.py:26
  176.7 13.5 %collective-permute-start.47 = (bf16[128,1024]{1,0:T(8,128)(2,1)S(1)}, bf16[128,1024]{1,0:T(8,128)(2,1)S(1)}, u32[]{:S(2)}, u32[]{:S(2)}) collective-permute-start(bf16[128,1024]{1,0:T(8,128)(2,1)S(1)} %get-tuple-element.89), channel_id=1, source_target_pairs={{0,4},{4,0},{1,5},{5,1},{2,6},{6,2},{3,7},{7,3},{8,12},{12,8},{9,1... | collective-permute-start | bytes 786440 | tf_op jit(solution)/shard_map/ppermute | solution.py:26
  178.2 28.5 %collective-permute-start.44 = (bf16[256,1024]{1,0:T(8,128)(2,1)}, bf16[256,1024]{1,0:T(8,128)(2,1)S(1)}, u32[]{:S(2)}, u32[]{:S(2)}) collective-permute-start(bf16[256,1024]{1,0:T(8,128)(2,1)} %get-tuple-element.80), channel_id=1, source_target_pairs={{0,1},{1,0},{2,3},{3,2},{4,5},{5,4},{6,7},{7,6},{8,9},{9,8},{10,11... | collective-permute-start | bytes 1572872 | tf_op jit(solution)/shard_map/ppermute | solution.py:26
  194.0 20.7 %collective-permute-start.57 = (bf16[128,1536]{1,0:T(8,128)(2,1)}, bf16[128,1536]{1,0:T(8,128)(2,1)}, u32[]{:S(2)}, u32[]{:S(2)}) collective-permute-start(bf16[128,1536]{1,0:T(8,128)(2,1)} %get-tuple-element.101), channel_id=1, source_target_pairs={{0,4},{4,0},{1,5},{5,1},{2,6},{6,2},{3,7},{7,3},{8,12},{12,8},{9,1... | collective-permute-start | bytes 1179656 | tf_op jit(solution)/shard_map/ppermute | solution.py:26
  194.6 6.5 %collective-permute-start.39 = (bf16[128,1024]{1,0:T(8,128)(2,1)S(1)}, bf16[128,1024]{1,0:T(8,128)(2,1)}, u32[]{:S(2)}, u32[]{:S(2)}) collective-permute-start(bf16[128,1024]{1,0:T(8,128)(2,1)S(1)} %onward.8.refs_23_), channel_id=1, source_target_pairs={{0,2},{2,0},{1,3},{3,1},{4,6},{6,4},{5,7},{7,5},{8,10},{10,8},{9,1... | collective-permute-start | bytes 786440 | tf_op jit(solution)/shard_map/ppermute | solution.py:26
  195.1 16.2 %collective-permute-start.50 = (bf16[128,1024]{1,0:T(8,128)(2,1)}, bf16[128,1024]{1,0:T(8,128)(2,1)}, u32[]{:S(2)}, u32[]{:S(2)}) collective-permute-start(bf16[128,1024]{1,0:T(8,128)(2,1)} %get-tuple-element.93), channel_id=1, source_target_pairs={{0,4},{4,0},{1,5},{5,1},{2,6},{6,2},{3,7},{7,3},{8,12},{12,8},{9,1... | collective-permute-start | bytes 786440 | tf_op jit(solution)/shard_map/ppermute | solution.py:26
  196.6 16.0 %collective-permute-start.51 = (bf16[128,1024]{1,0:T(8,128)(2,1)}, bf16[128,1024]{1,0:T(8,128)(2,1)}, u32[]{:S(2)}, u32[]{:S(2)}) collective-permute-start(bf16[128,1024]{1,0:T(8,128)(2,1)} %merge.7.refs_2_), channel_id=1, source_target_pairs={{0,8},{8,0},{16,24},{24,16},{1,9},{9,1},{17,25},{25,17},{2,10},{10... | collective-permute-start | bytes 786440 | tf_op jit(solution)/shard_map/ppermute | solution.py:72
  205.1 13.8 %collective-permute-start.46 = (bf16[128,1024]{1,0:T(8,128)(2,1)S(1)}, bf16[128,1024]{1,0:T(8,128)(2,1)S(1)}, u32[]{:S(2)}, u32[]{:S(2)}) collective-permute-start(bf16[128,1024]{1,0:T(8,128)(2,1)S(1)} %copy-done.57), channel_id=1, source_target_pairs={{0,4},{4,0},{1,5},{5,1},{2,6},{6,2},{3,7},{7,3},{8,12},{12,8},{9,1... | collective-permute-start | bytes 786440 | tf_op jit(solution)/shard_map/ppermute | solution.py:26
  206.7 13.4 %collective-permute-start.49 = (bf16[128,1024]{1,0:T(8,128)(2,1)S(1)}, bf16[128,1024]{1,0:T(8,128)(2,1)S(1)}, u32[]{:S(2)}, u32[]{:S(2)}) collective-permute-start(bf16[128,1024]{1,0:T(8,128)(2,1)S(1)} %merge.8.refs_3_), channel_id=1, source_target_pairs={{0,8},{8,0},{16,24},{24,16},{1,9},{9,1},{17,25},{25,17},{2,10},{10... | collective-permute-start | bytes 786440 | tf_op jit(solution)/shard_map/ppermute | solution.py:72
  211.2 14.8 %collective-permute-start.45 = (bf16[128,1024]{1,0:T(8,128)(2,1)S(1)}, bf16[128,1024]{1,0:T(8,128)(2,1)S(1)}, u32[]{:S(2)}, u32[]{:S(2)}) collective-permute-start(bf16[128,1024]{1,0:T(8,128)(2,1)S(1)} %onward.9), channel_id=1, source_target_pairs={{0,2},{2,0},{1,3},{3,1},{4,6},{6,4},{5,7},{7,5},{8,10},{10,8},{9,1... | collective-permute-start | bytes 786440 | tf_op jit(solution)/shard_map/ppermute | solution.py:26
  213.7 9.9 %collective-permute-start.52 = (bf16[128,1024]{1,0:T(8,128)(2,1)S(1)}, bf16[128,1024]{1,0:T(8,128)(2,1)S(1)}, u32[]{:S(2)}, u32[]{:S(2)}) collective-permute-start(bf16[128,1024]{1,0:T(8,128)(2,1)S(1)} %merge.9), channel_id=1, source_target_pairs={{0,16},{8,24},{16,0},{24,8},{1,17},{9,25},{17,1},{25,9},{2,18},{10... | collective-permute-start | bytes 786440 | tf_op jit(solution)/shard_map/ppermute | solution.py:72
  216.7 16.0 %collective-permute-start.58 = (bf16[128,1024]{1,0:T(8,128)(2,1)}, bf16[128,1024]{1,0:T(8,128)(2,1)}, u32[]{:S(2)}, u32[]{:S(2)}) collective-permute-start(bf16[128,1024]{1,0:T(8,128)(2,1)} %get-tuple-element.131), channel_id=1, source_target_pairs={{1,2},{2,1},{5,6},{6,5},{9,10},{10,9},{13,14},{14,13},{17,18},{18,... | collective-permute-start | bytes 786440 | tf_op jit(solution)/shard_map/ppermute | solution.py:957
  219.0 13.7 %collective-permute-start.59 = (bf16[128,1024]{1,0:T(8,128)(2,1)}, bf16[128,1024]{1,0:T(8,128)(2,1)}, u32[]{:S(2)}, u32[]{:S(2)}) collective-permute-start(bf16[128,1024]{1,0:T(8,128)(2,1)} %get-tuple-element.130), channel_id=1, source_target_pairs={{0,2},{1,0},{2,3},{3,1},{4,6},{5,4},{6,7},{7,5},{8,10},{9,8},{10,1... | collective-permute-start | bytes 786440 | tf_op jit(solution)/shard_map/ppermute | solution.py:958
  224.3 6.2 %collective-permute-start.53 = (bf16[128,256]{1,0:T(8,128)(2,1)S(1)}, bf16[128,256]{1,0:T(8,128)(2,1)S(1)}, u32[]{:S(2)}, u32[]{:S(2)}) collective-permute-start(bf16[128,256]{1,0:T(8,128)(2,1)S(1)} %broadcast_select_fusion.18), channel_id=1, source_target_pairs={{0,2},{2,0},{1,3},{3,1},{4,6},{6,4},{5,7},{7,5},{8,10},{10,8},{9,1... | collective-permute-start | bytes 196616 | tf_op jit(solution)/shard_map/ppermute | solution.py:26
  227.4 16.3 %all-to-all-start = ((bf16[32,48,128]{2,1,0:T(8,128)(2,1)}), bf16[32,48,128]{2,1,0:T(8,128)(2,1)S(1)}, u32[]{:S(2)}, u32[]{:S(2)}) async-start(bf16[32,48,128]{2,1,0:T(8,128)(2,1)} %get-tuple-element.83), calls=%async_computation | async-start | bytes 786432 | tf_op jit(solution)/shard_map/all_to_all | solution.py:918
  230.6 1.3 collective-permute-start.54
  (58 other events, 456.3 us)
